TPU v7x, 32 devices: a whole 2x2x4 slice. The times are simulated.
32 devices in a mesh: slab: 8 (over z, x), layer: 4 (over y, core).
Axes of the slice: x: 2, y: 2, z: 4, core: 2. Of those that a mesh axis runs over, the one named last changes fastest.
Arguments:
- adjoint_source: float32 [4, 128, 4096], P('layer', 'slab')
- conductivity: float32 [4, 128, 4096], P('layer', 'slab'), may hold values from 0.3 to 3
- tile_owner: int32 [1, 32], replicated, may hold values from 0 to 7, as said below
Outputs:
- adjoint: float32 [4, 128, 4096], P('layer', 'slab')
- owned_grad: float32 [32, 128, 128], P('slab', 'layer')
Inputs may be any that keep to these rules, and one draw needn't show every extreme that they name: `tile_owner`: every owner holds exactly 4 tiles, and in every row of tiles each owner holds at most 4 tile; in every row some owner holds 4 tile.
All inputs are finite; a program needn't handle non-finite values.
Results may differ from a plain program's by a relative error of at most 0.0003.
Values sent between devices are 32-bit elements; how exact they have to be, the bound alone decides.
A program may use at most 64 MiB of HBM per device.

v0:
```python
import jax
import jax.numpy as jnp
from jax import lax
from jax.sharding import PartitionSpec as P

TILE = 128
ITERS = 3


def padded_2(block, sides, width):
    for axis, dim in sides:
        count = lax.axis_size(axis)
        forward = [(i, i + 1) for i in range(count - 1)]
        backward = [(target, source) for source, target in forward]
        low = lax.ppermute(
            lax.slice_in_dim(block, block.shape[dim] - width, None, axis=dim), axis, forward
        )
        high = lax.ppermute(lax.slice_in_dim(block, 0, width, axis=dim), axis, backward)
        block = jnp.concatenate([low, block, high], axis=dim)
    return block


def neighbours(padded):
    return [
        padded[2:, 1:-1, 1:-1],
        padded[:-2, 1:-1, 1:-1],
        padded[1:-1, 2:, 1:-1],
        padded[1:-1, :-2, 1:-1],
        padded[1:-1, 1:-1, 2:],
        padded[1:-1, 1:-1, :-2],
    ]


def extend(field):
    framed = padded_2(field, (("slab", 1), ("layer", 0)), 1)
    return jnp.pad(framed, ((0, 0), (0, 0), (1, 1)))


def per_device(adjoint_source, conductivity, tile_owner):
    layer_depth, row_count, column_count = adjoint_source.shape
    slab_count = lax.axis_size("slab")
    face_conds = [
        0.5 * (conductivity + near_cond) for near_cond in neighbours(extend(conductivity))
    ]
    diagonal = jnp.zeros_like(conductivity)
    for face_cond in face_conds:
        diagonal = diagonal + face_cond
    inverse = 1.0 / diagonal
    solution = jnp.zeros_like(adjoint_source)
    residual = adjoint_source

    def combined(value):
        slab_total = lax.psum(value, "slab")
        return lax.psum(slab_total, "layer")

    precond = inverse * residual
    direction = precond
    inner_now = combined(jnp.sum(residual * precond))
    for iteration in range(ITERS):
        result = jnp.zeros_like(direction)
        for apply_face_cond, near_field in zip(face_conds, neighbours(extend(direction))):
            result = result + apply_face_cond * (direction - near_field)
        step_size = inner_now / combined(jnp.sum(direction * result))
        solution = solution + step_size * direction
        residual = residual - step_size * result
        if iteration + 1 < ITERS:
            precond = inverse * residual
            inner_next = combined(jnp.sum(residual * precond))
            direction = precond + inner_next / inner_now * direction
            inner_now = inner_next
    partial_map = jnp.sum(solution, axis=0)
    tiles_across = tile_owner.shape[1]
    tile_rows = tile_owner.shape[0]
    blocks = partial_map.reshape(row_count, tiles_across, TILE)
    owner_index = lax.axis_index("slab")
    per_tile = TILE // row_count
    capacity = max(1, tiles_across // slab_count)
    owned_count = tile_rows * tiles_across // slab_count
    same_owner = tile_owner[:, :, None] == tile_owner[:, None, :]
    earlier = jnp.arange(tiles_across)[None, :] < jnp.arange(tiles_across)[:, None]
    slot_table = jnp.sum((same_owner & earlier[None, :, :]).astype(jnp.int32), axis=2)
    my_row = owner_index // per_tile
    row_owner = lax.dynamic_index_in_dim(tile_owner, my_row, 0, keepdims=False)
    row_slot = lax.dynamic_index_in_dim(slot_table, my_row, 0, keepdims=False)
    select = (
        (row_owner[None, None, :] == jnp.arange(slab_count, dtype=jnp.int32)[:, None, None])
        & (row_slot[None, None, :] == jnp.arange(capacity, dtype=jnp.int32)[None, :, None])
    ).astype(jnp.float32)
    flat_owner = tile_owner.reshape(-1)
    flat_slot = slot_table.reshape(-1)
    flat_row = jnp.arange(tile_rows * tiles_across, dtype=jnp.int32) // tiles_across
    owned_flag = flat_owner == owner_index
    owned_rank = jnp.cumsum(owned_flag.astype(jnp.int32)) - 1
    picked = owned_flag[None, :] & (
        owned_rank[None, :] == jnp.arange(owned_count, dtype=jnp.int32)[:, None]
    )
    tile_row_of = jnp.sum(jnp.where(picked, flat_row[None, :], 0), axis=1)
    tile_slot_of = jnp.sum(jnp.where(picked, flat_slot[None, :], 0), axis=1)
    sender = tile_row_of[:, None] * per_tile + jnp.arange(per_tile, dtype=jnp.int32)[None, :]
    gather_sel = (
        (sender[:, :, None, None] == jnp.arange(slab_count, dtype=jnp.int32)[None, None, :, None])
        & (
            tile_slot_of[:, None, None, None]
            == jnp.arange(capacity, dtype=jnp.int32)[None, None, None, :]
        )
    ).astype(jnp.float32)
    strips = lax.psum_scatter(blocks, "layer", scatter_dimension=2, tiled=True)
    strip_width = strips.shape[2]
    outgoing = jnp.einsum("ojc,xcw->ojwx", select, strips, precision=lax.Precision.HIGHEST)
    outgoing = outgoing.reshape(slab_count, capacity, strip_width * row_count)
    received = lax.all_to_all(outgoing, "slab", split_axis=0, concat_axis=0, tiled=True)
    shaped = received.reshape(slab_count, capacity, strip_width, row_count)
    placed = jnp.einsum("kqsj,sjwx->kwqx", gather_sel, shaped, precision=lax.Precision.HIGHEST)
    owned_tiles = placed.reshape(owned_count, strip_width, TILE)
    return (solution, owned_tiles)


def solution(mesh):
    placed = (P("layer", "slab", None), P("layer", "slab", None), P())
    return jax.shard_map(
        per_device,
        mesh=mesh,
        in_specs=placed,
        out_specs=(P("layer", "slab", None), P("slab", "layer", None)),
        check_vma=False,
    )
```

profile of v0, /device:TPU:0, one launch (start us, length us, event | category | flops | bytes accessed | tf_op | source)
XLA Modules:
  0.0 280.8 jit_solution(12168273064981851369)
XLA Ops:
  7.2 1.0 fusion.69
  8.2 4.8 %collective-permute-start = (f32[1,1,4096]{2,1,0:T(1,128)S(1)}, f32[1,1,4096]{2,1,0:T(1,128)S(1)}, u32[]{:S(2)}, u32[]{:S(2)}) collective-permute-start(f32[1,1,4096]{2,1,0:T(1,128)S(1)} %get-tuple-element.30), channel_id=1, source_target_pairs={{0,4},{4,8},{8,12},{12,16},{16,20},{20,24},{24,28},{1,5},{5,9},{9,... | collective-permute-start | bytes 49160 | tf_op jit(solution)/shard_map/ppermute | solution.py:15
  13.1 1.3 collective-permute-start.1
  14.5 4.2 %collective-permute-done.1 = f32[1,1,4096]{2,1,0:T(1,128)S(1)} collective-permute-done((f32[1,1,4096]{2,1,0:T(1,128)S(1)}, f32[1,1,4096]{2,1,0:T(1,128)S(1)}, u32[]{:S(2)}, u32[]{:S(2)}) %collective-permute-start.1) | collective-permute-done | bytes 16416 | tf_op jit(solution)/shard_map/ppermute | solution.py:18
  18.7 1.0 pad_maximum_fusion
  19.7 1.4 collective-permute-start.2
  21.2 3.1 %collective-permute-start.3 = (f32[1,18,4096]{2,1,0:T(8,128)S(1)}, f32[1,18,4096]{2,1,0:T(8,128)S(1)}, u32[]{:S(2)}, u32[]{:S(2)}) collective-permute-start(f32[1,18,4096]{2,1,0:T(8,128)S(1)} %pad_maximum_fusion), channel_id=1, source_target_pairs={{0,1},{1,2},{2,3},{4,5},{5,6},{6,7},{8,9},{9,10},{10,11},{12,13},{... | collective-permute-start | bytes 884744 | tf_op jit(solution)/shard_map/ppermute | solution.py:15
  24.2 1.3 collective-permute-done.3
  25.5 1.4 select_maximum_fusion.12
  26.9 0.3 fusion.65
  27.3 4.4 %collective-permute-start.4 = (f32[1,1,4096]{2,1,0:T(1,128)S(1)}, f32[1,1,4096]{2,1,0:T(1,128)S(1)}, u32[]{:S(2)}, u32[]{:S(2)}) collective-permute-start(f32[1,1,4096]{2,1,0:T(1,128)S(1)} %get-tuple-element.28), channel_id=1, source_target_pairs={{0,4},{4,8},{8,12},{12,16},{16,20},{20,24},{24,28},{1,5},{5,9},{9,... | collective-permute-start | bytes 49160 | tf_op jit(solution)/shard_map/ppermute | solution.py:15
  31.7 1.3 collective-permute-start.5
  33.1 4.2 %collective-permute-done.5 = f32[1,1,4096]{2,1,0:T(1,128)S(1)} collective-permute-done((f32[1,1,4096]{2,1,0:T(1,128)S(1)}, f32[1,1,4096]{2,1,0:T(1,128)S(1)}, u32[]{:S(2)}, u32[]{:S(2)}) %collective-permute-start.5) | collective-permute-done | bytes 16416 | tf_op jit(solution)/shard_map/ppermute | solution.py:18
  37.3 1.3 collective-permute-start.6
  38.6 5.6 %collective-permute-start.7 = (f32[1,18,4096]{2,1,0:T(8,128)S(1)}, f32[1,18,4096]{2,1,0:T(8,128)S(1)}, u32[]{:S(2)}, u32[]{:S(2)}) collective-permute-start(f32[1,18,4096]{2,1,0:T(8,128)S(1)} %pad_maximum_fusion.1), channel_id=1, source_target_pairs={{0,1},{1,2},{2,3},{4,5},{5,6},{6,7},{8,9},{9,10},{10,11},{12,13},{... | collective-permute-start | bytes 884744 | tf_op jit(solution)/shard_map/ppermute | solution.py:15
  44.3 1.3 collective-permute-done.7
  45.6 0.4 select_maximum_fusion.8
  46.0 1.2 multiply_reduce_fusion.3
  47.2 19.5 %all-reduce.4 = (f32[]{:T(128)}, f32[]{:T(128)}) all-reduce(f32[]{:T(128)} %get-tuple-element.9, f32[]{:T(128)} %get-tuple-element.8), channel_id=1, replica_groups=mesh['slab'=8,'layer'=4] {'slab'}, use_global_device_ids=true, to_apply=%region_1.2 | all-reduce | flops 2 | bytes 16 | tf_op jit(solution)/shard_map/psum | solution.py:53
  66.7 13.9 %all-reduce.5 = (f32[]{:T(128)}, f32[]{:T(128)}) all-reduce(f32[]{:T(128)} %get-tuple-element.12, f32[]{:T(128)} %get-tuple-element.13), channel_id=1, replica_groups=mesh['slab'=8,'layer'=4] {'layer'}, use_global_device_ids=true, to_apply=%region_2.3 | all-reduce | flops 2 | bytes 16 | tf_op jit(solution)/shard_map/psum | solution.py:54
  81.9 1.4 multiply_reduce_fusion.2
  83.3 18.0 %psum.88 = f32[]{:T(128)} all-reduce(f32[]{:T(128)} %get-tuple-element.18), channel_id=1, replica_groups=mesh['slab'=8,'layer'=4] {'slab'}, use_global_device_ids=true, to_apply=%region_7.8 | all-reduce | flops 1 | bytes 8 | tf_op jit(solution)/shard_map/psum | solution.py:53
  101.4 6.4 %psum.89 = f32[]{:T(128)} all-reduce(f32[]{:T(128)} %psum.88), channel_id=1, replica_groups=mesh['slab'=8,'layer'=4] {'layer'}, use_global_device_ids=true, to_apply=%region_8.9 | all-reduce | flops 1 | bytes 8 | tf_op jit(solution)/shard_map/psum | solution.py:54
  109.0 1.0 multiply_add_fusion.2
  110.1 3.6 %collective-permute-start.8 = (f32[1,1,4096]{2,1,0:T(1,128)S(1)}, f32[1,1,4096]{2,1,0:T(1,128)S(1)}, u32[]{:S(2)}, u32[]{:S(2)}) collective-permute-start(f32[1,1,4096]{2,1,0:T(1,128)S(1)} %get-tuple-element.26), channel_id=1, source_target_pairs={{0,4},{4,8},{8,12},{12,16},{16,20},{20,24},{24,28},{1,5},{5,9},{9,... | collective-permute-start | bytes 49160 | tf_op jit(solution)/shard_map/ppermute | solution.py:15
  113.7 1.3 collective-permute-start.9
  115.1 4.2 %collective-permute-done.9 = f32[1,1,4096]{2,1,0:T(1,128)S(1)} collective-permute-done((f32[1,1,4096]{2,1,0:T(1,128)S(1)}, f32[1,1,4096]{2,1,0:T(1,128)S(1)}, u32[]{:S(2)}, u32[]{:S(2)}) %collective-permute-start.9) | collective-permute-done | bytes 16416 | tf_op jit(solution)/shard_map/ppermute | solution.py:18
  119.4 1.3 collective-permute-start.10
  120.7 3.1 %collective-permute-start.11 = (f32[1,18,4096]{2,1,0:T(8,128)S(1)}, f32[1,18,4096]{2,1,0:T(8,128)S(1)}, u32[]{:S(2)}, u32[]{:S(2)}) collective-permute-start(f32[1,18,4096]{2,1,0:T(8,128)S(1)} %pad_maximum_fusion.2), channel_id=1, source_target_pairs={{0,1},{1,2},{2,3},{4,5},{5,6},{6,7},{8,9},{9,10},{10,11},{12,13},{... | collective-permute-start | bytes 884744 | tf_op jit(solution)/shard_map/ppermute | solution.py:15
  123.8 0.2 convert_reduce_fusion
  124.0 1.1 collective-permute-done.11
  125.1 0.5 select_maximum_fusion.4
  125.5 1.2 multiply_reduce_fusion.1
  126.7 18.7 %psum.90 = f32[]{:T(128)} all-reduce(f32[]{:T(128)} %get-tuple-element.16), channel_id=1, replica_groups=mesh['slab'=8,'layer'=4] {'slab'}, use_global_device_ids=true, to_apply=%region_10.11 | all-reduce | flops 1 | bytes 8 | tf_op jit(solution)/shard_map/psum | solution.py:53
  145.4 11.7 %psum.91 = f32[]{:T(128)} all-reduce(f32[]{:T(128)} %psum.90), channel_id=1, replica_groups=mesh['slab'=8,'layer'=4] {'layer'}, use_global_device_ids=true, to_apply=%region_11.12 | all-reduce | flops 1 | bytes 8 | tf_op jit(solution)/shard_map/psum | solution.py:54
  158.5 1.7 multiply_reduce_fusion
  160.2 18.9 %psum.92 = f32[]{:T(128)} all-reduce(f32[]{:T(128)} %multiply_reduce_fusion), channel_id=1, replica_groups=mesh['slab'=8,'layer'=4] {'slab'}, use_global_device_ids=true, to_apply=%region_13.14 | all-reduce | flops 1 | bytes 8 | tf_op jit(solution)/shard_map/psum | solution.py:53
  179.1 6.4 %psum.93 = f32[]{:T(128)} all-reduce(f32[]{:T(128)} %psum.92), channel_id=1, replica_groups=mesh['slab'=8,'layer'=4] {'layer'}, use_global_device_ids=true, to_apply=%region_14.15 | all-reduce | flops 1 | bytes 8 | tf_op jit(solution)/shard_map/psum | solution.py:54
  186.8 1.1 multiply_add_fusion.1
  188.0 2.9 %collective-permute-start.12 = (f32[1,1,4096]{2,1,0:T(1,128)S(1)}, f32[1,1,4096]{2,1,0:T(1,128)S(1)}, u32[]{:S(2)}, u32[]{:S(2)}) collective-permute-start(f32[1,1,4096]{2,1,0:T(1,128)S(1)} %get-tuple-element.24), channel_id=1, source_target_pairs={{0,4},{4,8},{8,12},{12,16},{16,20},{20,24},{24,28},{1,5},{5,9},{9,... | collective-permute-start | bytes 49160 | tf_op jit(solution)/shard_map/ppermute | solution.py:15
  190.8 1.3 collective-permute-start.13
  192.3 4.2 %collective-permute-done.13 = f32[1,1,4096]{2,1,0:T(1,128)S(1)} collective-permute-done((f32[1,1,4096]{2,1,0:T(1,128)S(1)}, f32[1,1,4096]{2,1,0:T(1,128)S(1)}, u32[]{:S(2)}, u32[]{:S(2)}) %collective-permute-start.13) | collective-permute-done | bytes 16416 | tf_op jit(solution)/shard_map/ppermute | solution.py:18
  196.5 1.3 collective-permute-start.14
  197.8 3.1 %collective-permute-start.15 = (f32[1,18,4096]{2,1,0:T(8,128)S(1)}, f32[1,18,4096]{2,1,0:T(8,128)S(1)}, u32[]{:S(2)}, u32[]{:S(2)}) collective-permute-start(f32[1,18,4096]{2,1,0:T(8,128)S(1)} %pad_maximum_fusion.3), channel_id=1, source_target_pairs={{0,1},{1,2},{2,3},{4,5},{5,6},{6,7},{8,9},{9,10},{10,11},{12,13},{... | collective-permute-start | bytes 884744 | tf_op jit(solution)/shard_map/ppermute | solution.py:15
  201.0 1.2 collective-permute-done.15
  202.2 0.5 select_maximum_fusion
  202.7 1.2 fusion.4
  203.8 18.7 %psum.94 = f32[]{:T(128)} all-reduce(f32[]{:T(128)} %fusion.4), channel_id=1, replica_groups=mesh['slab'=8,'layer'=4] {'slab'}, use_global_device_ids=true, to_apply=%region_16.17 | all-reduce | flops 1 | bytes 8 | tf_op jit(solution)/shard_map/psum | solution.py:53
  222.7 11.7 %psum.95 = f32[]{:T(128)} all-reduce(f32[]{:T(128)} %psum.94), channel_id=1, replica_groups=mesh['slab'=8,'layer'=4] {'layer'}, use_global_device_ids=true, to_apply=%region_17.18 | all-reduce | flops 1 | bytes 8 | tf_op jit(solution)/shard_map/psum | solution.py:54
  235.7 1.2 multiply_add_fusion
  236.9 0.5 copy.33
  237.4 1.1 reshape.263
  238.7 18.6 %reduce-scatter.4.cloned.1.call-done = f32[32,512]{1,0:T(8,128)} async-done(((f32[128,512]{1,0:T(8,128)}), f32[32,512]{1,0:T(8,128)}) %reduce-scatter.4.cloned.1.call-update) | async-done | bytes 65552
  257.2 0.9 reshape.264
  258.2 0.2 copy.34
  258.3 0.3 convolution_bitcast_fusion.1
  258.6 0.2 copy.28
  258.9 0.9 reshape.261
  259.8 5.5 %all-to-all-start = ((f32[8,4,512]{2,1,0:T(4,128)}), f32[8,4,512]{2,1,0:T(4,128)S(1)}, u32[]{:S(2)}, u32[]{:S(2)}) async-start(f32[8,4,512]{2,1,0:T(4,128)} %reshape.261), calls=%async_computation | async-start | bytes 131072 | tf_op jit(solution)/shard_map/all_to_all | solution.py:111
  265.4 6.8 %all-to-all-done = f32[8,4,512]{2,1,0:T(4,128)S(1)} async-done(((f32[8,4,512]{2,1,0:T(4,128)}), f32[8,4,512]{2,1,0:T(4,128)S(1)}, u32[]{:S(2)}, u32[]{:S(2)}) %all-to-all-start) | async-done | bytes 65568 | tf_op jit(solution)/shard_map/all_to_all | solution.py:111
  272.2 0.2 reshape.262
  272.4 0.3 copy.26
  272.7 0.4 convolution_bitcast_fusion
  273.2 0.7 copy.24
  (40 shorter events, 1.6 us)
Async XLA Ops:
  7.2 250.1 %reduce-scatter.4.cloned.1.call-start = ((), (), s32[]{:S(2)}) async-start(), calls=%async_computation.2 | async-start | bytes 327680
  8.2 6.3 %collective-permute-start = (f32[1,1,4096]{2,1,0:T(1,128)S(1)}, f32[1,1,4096]{2,1,0:T(1,128)S(1)}, u32[]{:S(2)}, u32[]{:S(2)}) collective-permute-start(f32[1,1,4096]{2,1,0:T(1,128)S(1)} %get-tuple-element.30), channel_id=1, source_target_pairs={{0,4},{4,8},{8,12},{12,16},{16,20},{20,24},{24,28},{1,5},{5,9},{9,... | collective-permute-start | bytes 49160 | tf_op jit(solution)/shard_map/ppermute | solution.py:15
  13.1 5.6 %collective-permute-start.1 = (f32[1,1,4096]{2,1,0:T(1,128)S(1)}, f32[1,1,4096]{2,1,0:T(1,128)S(1)}, u32[]{:S(2)}, u32[]{:S(2)}) collective-permute-start(f32[1,1,4096]{2,1,0:T(1,128)S(1)} %get-tuple-element.31), channel_id=1, source_target_pairs={{4,0},{8,4},{12,8},{16,12},{20,16},{24,20},{28,24},{5,1},{9,5},{13... | collective-permute-start | bytes 49160 | tf_op jit(solution)/shard_map/ppermute | solution.py:18
  19.7 7.2 %copy-start = (f32[1,16,4096]{2,1,0:T(8,128)S(1)}, f32[1,16,4096]{2,1,0:T(8,128)}, u32[]{:S(2)}) copy-start(f32[1,16,4096]{2,1,0:T(8,128)} %param.4) | copy-start | bytes 786436
  19.7 7.2 %copy-start.2 = (f32[1,16,4096]{2,1,0:T(8,128)S(1)}, f32[1,16,4096]{2,1,0:T(8,128)}, u32[]{:S(2)}) copy-start(f32[1,16,4096]{2,1,0:T(8,128)} %param.3) | copy-start | bytes 786436
  19.7 4.5 %collective-permute-start.2 = (f32[1,18,4096]{2,1,0:T(8,128)S(1)}, f32[1,18,4096]{2,1,0:T(8,128)S(1)}, u32[]{:S(2)}, u32[]{:S(2)}) collective-permute-start(f32[1,18,4096]{2,1,0:T(8,128)S(1)} %pad_maximum_fusion), channel_id=1, source_target_pairs={{1,0},{2,1},{3,2},{5,4},{6,5},{7,6},{9,8},{10,9},{11,10},{13,12},{... | collective-permute-start | bytes 884744 | tf_op jit(solution)/shard_map/ppermute | solution.py:18
  21.2 4.4 %collective-permute-start.3 = (f32[1,18,4096]{2,1,0:T(8,128)S(1)}, f32[1,18,4096]{2,1,0:T(8,128)S(1)}, u32[]{:S(2)}, u32[]{:S(2)}) collective-permute-start(f32[1,18,4096]{2,1,0:T(8,128)S(1)} %pad_maximum_fusion), channel_id=1, source_target_pairs={{0,1},{1,2},{2,3},{4,5},{5,6},{6,7},{8,9},{9,10},{10,11},{12,13},{... | collective-permute-start | bytes 884744 | tf_op jit(solution)/shard_map/ppermute | solution.py:15
  27.3 5.8 %collective-permute-start.4 = (f32[1,1,4096]{2,1,0:T(1,128)S(1)}, f32[1,1,4096]{2,1,0:T(1,128)S(1)}, u32[]{:S(2)}, u32[]{:S(2)}) collective-permute-start(f32[1,1,4096]{2,1,0:T(1,128)S(1)} %get-tuple-element.28), channel_id=1, source_target_pairs={{0,4},{4,8},{8,12},{12,16},{16,20},{20,24},{24,28},{1,5},{5,9},{9,... | collective-permute-start | bytes 49160 | tf_op jit(solution)/shard_map/ppermute | solution.py:15
  31.7 5.6 %collective-permute-start.5 = (f32[1,1,4096]{2,1,0:T(1,128)S(1)}, f32[1,1,4096]{2,1,0:T(1,128)S(1)}, u32[]{:S(2)}, u32[]{:S(2)}) collective-permute-start(f32[1,1,4096]{2,1,0:T(1,128)S(1)} %get-tuple-element.29), channel_id=1, source_target_pairs={{4,0},{8,4},{12,8},{16,12},{20,16},{24,20},{28,24},{5,1},{9,5},{13... | collective-permute-start | bytes 49160 | tf_op jit(solution)/shard_map/ppermute | solution.py:18
  37.3 6.9 %collective-permute-start.6 = (f32[1,18,4096]{2,1,0:T(8,128)S(1)}, f32[1,18,4096]{2,1,0:T(8,128)S(1)}, u32[]{:S(2)}, u32[]{:S(2)}) collective-permute-start(f32[1,18,4096]{2,1,0:T(8,128)S(1)} %pad_maximum_fusion.1), channel_id=1, source_target_pairs={{1,0},{2,1},{3,2},{5,4},{6,5},{7,6},{9,8},{10,9},{11,10},{13,12},{... | collective-permute-start | bytes 884744 | tf_op jit(solution)/shard_map/ppermute | solution.py:18
  38.6 7.0 %collective-permute-start.7 = (f32[1,18,4096]{2,1,0:T(8,128)S(1)}, f32[1,18,4096]{2,1,0:T(8,128)S(1)}, u32[]{:S(2)}, u32[]{:S(2)}) collective-permute-start(f32[1,18,4096]{2,1,0:T(8,128)S(1)} %pad_maximum_fusion.1), channel_id=1, source_target_pairs={{0,1},{1,2},{2,3},{4,5},{5,6},{6,7},{8,9},{9,10},{10,11},{12,13},{... | collective-permute-start | bytes 884744 | tf_op jit(solution)/shard_map/ppermute | solution.py:15
  81.9 41.9 %copy-start.4 = (s32[1,32]{1,0:T(1,128)S(1)}, s32[1,32]{1,0:T(1,128)}, u32[]{:S(2)}) copy-start(s32[1,32]{1,0:T(1,128)} %param.5) | copy-start | bytes 388
  110.1 5.1 %collective-permute-start.8 = (f32[1,1,4096]{2,1,0:T(1,128)S(1)}, f32[1,1,4096]{2,1,0:T(1,128)S(1)}, u32[]{:S(2)}, u32[]{:S(2)}) collective-permute-start(f32[1,1,4096]{2,1,0:T(1,128)S(1)} %get-tuple-element.26), channel_id=1, source_target_pairs={{0,4},{4,8},{8,12},{12,16},{16,20},{20,24},{24,28},{1,5},{5,9},{9,... | collective-permute-start | bytes 49160 | tf_op jit(solution)/shard_map/ppermute | solution.py:15
  113.7 5.6 %collective-permute-start.9 = (f32[1,1,4096]{2,1,0:T(1,128)S(1)}, f32[1,1,4096]{2,1,0:T(1,128)S(1)}, u32[]{:S(2)}, u32[]{:S(2)}) collective-permute-start(f32[1,1,4096]{2,1,0:T(1,128)S(1)} %get-tuple-element.27), channel_id=1, source_target_pairs={{4,0},{8,4},{12,8},{16,12},{20,16},{24,20},{28,24},{5,1},{9,5},{13... | collective-permute-start | bytes 49160 | tf_op jit(solution)/shard_map/ppermute | solution.py:18
  119.4 4.6 %collective-permute-start.10 = (f32[1,18,4096]{2,1,0:T(8,128)S(1)}, f32[1,18,4096]{2,1,0:T(8,128)S(1)}, u32[]{:S(2)}, u32[]{:S(2)}) collective-permute-start(f32[1,18,4096]{2,1,0:T(8,128)S(1)} %pad_maximum_fusion.2), channel_id=1, source_target_pairs={{1,0},{2,1},{3,2},{5,4},{6,5},{7,6},{9,8},{10,9},{11,10},{13,12},{... | collective-permute-start | bytes 884744 | tf_op jit(solution)/shard_map/ppermute | solution.py:18
  120.7 4.4 %collective-permute-start.11 = (f32[1,18,4096]{2,1,0:T(8,128)S(1)}, f32[1,18,4096]{2,1,0:T(8,128)S(1)}, u32[]{:S(2)}, u32[]{:S(2)}) collective-permute-start(f32[1,18,4096]{2,1,0:T(8,128)S(1)} %pad_maximum_fusion.2), channel_id=1, source_target_pairs={{0,1},{1,2},{2,3},{4,5},{5,6},{6,7},{8,9},{9,10},{10,11},{12,13},{... | collective-permute-start | bytes 884744 | tf_op jit(solution)/shard_map/ppermute | solution.py:15
  126.7 58.8 %copy-start.1 = (f32[1,16,4096]{2,1,0:T(8,128)}, f32[1,16,4096]{2,1,0:T(8,128)S(1)}, u32[]{:S(2)}) copy-start(f32[1,16,4096]{2,1,0:T(8,128)S(1)} %get-tuple-element.17) | copy-start | bytes 786436
  188.0 4.3 %collective-permute-start.12 = (f32[1,1,4096]{2,1,0:T(1,128)S(1)}, f32[1,1,4096]{2,1,0:T(1,128)S(1)}, u32[]{:S(2)}, u32[]{:S(2)}) collective-permute-start(f32[1,1,4096]{2,1,0:T(1,128)S(1)} %get-tuple-element.24), channel_id=1, source_target_pairs={{0,4},{4,8},{8,12},{12,16},{16,20},{20,24},{24,28},{1,5},{5,9},{9,... | collective-permute-start | bytes 49160 | tf_op jit(solution)/shard_map/ppermute | solution.py:15
  190.8 5.6 %collective-permute-start.13 = (f32[1,1,4096]{2,1,0:T(1,128)S(1)}, f32[1,1,4096]{2,1,0:T(1,128)S(1)}, u32[]{:S(2)}, u32[]{:S(2)}) collective-permute-start(f32[1,1,4096]{2,1,0:T(1,128)S(1)} %get-tuple-element.25), channel_id=1, source_target_pairs={{4,0},{8,4},{12,8},{16,12},{20,16},{24,20},{28,24},{5,1},{9,5},{13... | collective-permute-start | bytes 49160 | tf_op jit(solution)/shard_map/ppermute | solution.py:18
  196.5 4.5 %collective-permute-start.14 = (f32[1,18,4096]{2,1,0:T(8,128)S(1)}, f32[1,18,4096]{2,1,0:T(8,128)S(1)}, u32[]{:S(2)}, u32[]{:S(2)}) collective-permute-start(f32[1,18,4096]{2,1,0:T(8,128)S(1)} %pad_maximum_fusion.3), channel_id=1, source_target_pairs={{1,0},{2,1},{3,2},{5,4},{6,5},{7,6},{9,8},{10,9},{11,10},{13,12},{... | collective-permute-start | bytes 884744 | tf_op jit(solution)/shard_map/ppermute | solution.py:18
  197.8 4.4 %collective-permute-start.15 = (f32[1,18,4096]{2,1,0:T(8,128)S(1)}, f32[1,18,4096]{2,1,0:T(8,128)S(1)}, u32[]{:S(2)}, u32[]{:S(2)}) collective-permute-start(f32[1,18,4096]{2,1,0:T(8,128)S(1)} %pad_maximum_fusion.3), channel_id=1, source_target_pairs={{0,1},{1,2},{2,3},{4,5},{5,6},{6,7},{8,9},{9,10},{10,11},{12,13},{... | collective-permute-start | bytes 884744 | tf_op jit(solution)/shard_map/ppermute | solution.py:15
  236.9 1.6 copy-start.3
  259.8 12.4 %all-to-all-start = ((f32[8,4,512]{2,1,0:T(4,128)}), f32[8,4,512]{2,1,0:T(4,128)S(1)}, u32[]{:S(2)}, u32[]{:S(2)}) async-start(f32[8,4,512]{2,1,0:T(4,128)} %reshape.261), calls=%async_computation | async-start | bytes 131072 | tf_op jit(solution)/shard_map/all_to_all | solution.py:111
Sparse Core Ops, SparseCore 0:
  238.6 18.5 reduce-scatter.3
where the time goes:
time: 282 us; the launch traced here: 281 us
  blocking collectives  144 us (51%)
  waiting for transfers between devices  47.4 us (17%)
  starting transfers between devices  46.5 us (16%)
  between operations  21 us (7%)
  other arithmetic  14.9 us (5%)
  local copies, waits for them, and re-layouts  6.42 us (2%)
    psum x5, blocking collectives, combined(): slab_total = lax.psum(value, 'slab')  93.8 us
    psum x5, blocking collectives, combined(): return lax.psum(slab_total, 'layer')  50.1 us
    ppermute x8, starting transfers between devices, padded_2(): lax.ppermute(lax.slice_in_dim(block, block.shape[dim] - width, None, axis...  30.5 us
    unnamed x2, waiting for transfers between devices  18.6 us
    ppermute x8, waiting for transfers between devices, padded_2(): lax.ppermute(lax.slice_in_dim(block, 0, width, axis=dim), axis, backward)  16.8 us
    ppermute x8, starting transfers between devices, padded_2(): lax.ppermute(lax.slice_in_dim(block, 0, width, axis=dim), axis, backward)  10.5 us
    all_to_all x1, waiting for transfers between devices, per_device(): lax.all_to_all(outgoing, 'slab', split_axis=0, concat_axis=0, tiled=True)  6.83 us
  transfers between devices with their start and end apart: 18, of which 13 were waited for; matrix products, arithmetic and copies ran while one was open for 0% of the time, Pallas kernels for 0%

commit v1 on v0

v1 whole, which is shorter than its diff:
```python
import functools

import jax
import jax.numpy as jnp
from jax import lax
from jax.experimental import pallas as pl
from jax.experimental.pallas import tpu as pltpu
from jax.sharding import PartitionSpec as P

TILE = 128
ITERS = 3
CHUNKS = 4
PAD = 128
MESH = pl.DeviceIdType.MESH


def fold(value):
    rows = sum(value[i : i + 8] for i in range(0, value.shape[0], 8))
    return sum(rows[:, i : i + 128] for i in range(0, value.shape[1], 128))


def cg_coefficients(mu):
    def inner(a, b):
        total = None
        for k in range(len(a) + len(b) - 1):
            coef = None
            for i in range(len(a)):
                if 0 <= k - i < len(b):
                    term = a[i] * b[k - i]
                    coef = term if coef is None else coef + term
            total = coef * mu[k] if total is None else total + coef * mu[k]
        return total

    def axpy(a, s, b):
        out = []
        for i in range(max(len(a), len(b))):
            if i >= len(b):
                out.append(a[i])
            elif i >= len(a):
                out.append(s * b[i])
            else:
                out.append(a[i] + s * b[i])
        return out

    one = jnp.ones_like(mu[0])
    zero = jnp.zeros_like(mu[0])
    sol, res, direction, now = [zero], [one], [one], mu[0]
    for iteration in range(ITERS):
        image = axpy(direction + [zero], -one, [zero] + direction)
        step = now / inner(direction, image)
        sol = axpy(sol, step, direction)
        if iteration + 1 < ITERS:
            res = axpy(res, -step, image)
            new = inner(res, res)
            direction = axpy(res, new / now, direction)
            now = new
    return sol


def kernel(
    n_slab,
    n_layer,
    src_ref,
    cond_ref,
    owner_ref,
    x_out,
    g_out,
    fields,
    coefs,
    inv_ref,
    layer_halo,
    row_send,
    row_recv,
    red_layer,
    red_slab,
    x_buf,
    x_tiles,
    strip_send,
    strip_recv,
    tile_send,
    tile_recv,
    table,
    halo_ssem,
    halo_rsem,
    red_ssem,
    red_rsem,
    strip_ssem,
    strip_rsem,
    tile_ssem,
    tile_rsem,
    out_sem,
):
    slab = lax.axis_index("slab")
    layer = lax.axis_index("layer")
    rows, cols = src_ref.shape[1], src_ref.shape[2]
    width = cols // CHUNKS
    top, bottom = 8, 8 + rows
    tile_rows, tiles_across = owner_ref.shape
    strip = TILE // n_layer
    capacity = max(1, tiles_across // n_slab)
    owned_count = g_out.shape[0]
    per_tile = TILE // rows

    def peers(axis, me, count):
        return [(d, {axis: lax.rem(me + d, count)}, lax.rem(me + count - d, count)) for d in range(1, count)]

    layer_peers = peers("layer", layer, n_layer)
    slab_peers = peers("slab", slab, n_slab)

    barrier = pltpu.get_barrier_semaphore()
    for _, device, _ in layer_peers + slab_peers:
        pl.semaphore_signal(barrier, inc=1, device_id=device, device_id_type=MESH)

    for s in range(4):
        fields[s, :, 0:PAD] = jnp.zeros((rows + 16, PAD), jnp.float32)
        fields[s, :, PAD + cols :] = jnp.zeros((rows + 16, PAD), jnp.float32)
    for d, axis_end in enumerate((layer == 0, layer == n_layer - 1)):

        @pl.when(axis_end)
        def _():
            for s in range(4):
                layer_halo[s, d] = jnp.zeros((rows, cols), jnp.float32)

    for d, axis_end in enumerate((slab == 0, slab == n_slab - 1)):

        @pl.when(axis_end)
        def _():
            for s in range(4):
                for j in range(CHUNKS):
                    row_recv[s, d, j] = jnp.zeros((1, width), jnp.float32)

    sends_to = (layer < n_layer - 1, layer > 0, slab < n_slab - 1, slab > 0)
    gets_from = (layer > 0, layer < n_layer - 1, slab > 0, slab < n_slab - 1)
    target = (
        {"layer": lax.rem(layer + 1, n_layer)},
        {"layer": lax.rem(layer + n_layer - 1, n_layer)},
        {"slab": lax.rem(slab + 1, n_slab)},
        {"slab": lax.rem(slab + n_slab - 1, n_slab)},
    )

    def used(stage, direction, j):
        if stage < 3:
            return True
        if direction == 0:
            return j < CHUNKS // 2
        if direction == 1:
            return j >= CHUNKS // 2
        return direction == 2

    def halo_copy(stage, direction, j):
        span = pl.ds(j * width, width)
        if direction < 2:
            source = fields.at[stage, pl.ds(top, rows), pl.ds(PAD + j * width, width)]
            dest = layer_halo.at[stage, direction, :, span]
        else:
            source = row_send.at[stage, direction - 2, j]
            dest = row_recv.at[stage, direction - 2, j]
        return pltpu.make_async_remote_copy(
            src_ref=source,
            dst_ref=dest,
            send_sem=halo_ssem.at[stage, direction, j],
            recv_sem=halo_rsem.at[stage, direction, j],
            device_id=target[direction],
            device_id_type=MESH,
        )

    def put_field(stage, j, value):
        fields[stage, top:bottom, PAD + j * width : PAD + (j + 1) * width] = value
        row_send[stage, 0, j] = value[rows - 1 : rows]
        row_send[stage, 1, j] = value[0:1]

    def send_field(stage, j):
        for direction in range(4):
            if used(stage, direction, j):

                @pl.when(sends_to[direction])
                def _():
                    halo_copy(stage, direction, j).start()

    def get_halo(stage, j):
        for direction in range(4):
            if used(stage, direction, j):

                @pl.when(gets_from[direction])
                def _():
                    halo_copy(stage, direction, j).wait_recv()

        span = slice(PAD + j * width, PAD + (j + 1) * width)
        fields[stage, top - 1 : top, span] = row_recv[stage, 0, j]
        if stage < 3:
            fields[stage, bottom : bottom + 1, span] = row_recv[stage, 1, j]

    def near(stage, j, which):
        c0 = j * width
        if which == "west":
            ext = fields[stage, top:bottom, c0 : c0 + width + 2 * PAD]
            return pltpu.roll(ext, 1, 1)[:, PAD : PAD + width]
        if which == "east":
            ext = fields[stage, top:bottom, c0 : c0 + width + 2 * PAD]
            return pltpu.roll(ext, width + 2 * PAD - 1, 1)[:, PAD : PAD + width]
        span = slice(PAD + c0, PAD + c0 + width)
        if which == "north":
            return fields[stage, top - 1 : bottom - 1, span]
        if which == "south":
            return fields[stage, top + 1 : bottom + 1, span]
        return layer_halo[stage, 0 if which == "below" else 1, :, c0 : c0 + width]

    names = ("west", "east", "north", "south", "below", "above")

    def here(stage, j):
        return fields[stage, top:bottom, PAD + j * width : PAD + (j + 1) * width]

    for j in range(CHUNKS):
        put_field(0, j, cond_ref[0, :, j * width : (j + 1) * width])
    pl.semaphore_wait(barrier, n_layer + n_slab - 2)
    for j in range(CHUNKS):
        send_field(0, j)

    my_row = slab // per_tile

    def list_tiles(owner, carry):
        packed = jnp.int32(0)
        for t in range(tiles_across):
            packed = jnp.where(owner_ref[my_row, t] == owner, packed * 256 + t, packed)
        table[owner] = packed
        return carry

    lax.fori_loop(0, n_slab, list_tiles, 0)

    moments = [jnp.zeros((8, 128), jnp.float32) for _ in range(6)]
    for j in range(CHUNKS):
        get_halo(0, j)
        span = slice(j * width, (j + 1) * width)
        cond = here(0, j)
        diagonal = None
        for i, name in enumerate(names):
            face = cond + near(0, j, name)
            coefs[i, :, span] = face
            diagonal = face if diagonal is None else diagonal + face
        inverse = 1.0 / diagonal
        inv_ref[:, span] = inverse
        source = src_ref[0, :, span]
        field = source * inverse
        put_field(1, j, field)
        send_field(1, j)
        moments[0] = moments[0] + fold(field * source)
    for stage in (1, 2):
        for j in range(CHUNKS):
            get_halo(stage, j)
            span = slice(j * width, (j + 1) * width)
            image = None
            for i, name in enumerate(names):
                term = coefs[i, :, span] * near(stage, j, name)
                image = term if image is None else image + term
            field = inv_ref[:, span] * image
            put_field(stage + 1, j, field)
            send_field(stage + 1, j)
            moments[2 * stage - 1] = moments[2 * stage - 1] + fold(here(stage, j) * image)
            moments[2 * stage] = moments[2 * stage] + fold(field * image)
    for j in range(CHUNKS):
        get_halo(3, j)
        span = slice(j * width, (j + 1) * width)
        side = "below" if j < CHUNKS // 2 else "above"
        image = None
        for name in ("west", "north", side):
            term = coefs[names.index(name), :, span] * near(3, j, name)
            image = term if image is None else image + term
        moments[5] = moments[5] + fold(here(3, j) * image)
    moments[5] = 2.0 * moments[5]

    def exchange(peer_list, me, send_of, recv_buf, ssem, rsem):
        copies = []
        for d, device, _ in peer_list:
            copy = pltpu.make_async_remote_copy(
                src_ref=send_of(d, device),
                dst_ref=recv_buf.at[me],
                send_sem=ssem.at[d],
                recv_sem=rsem.at[d],
                device_id=device,
                device_id_type=MESH,
            )
            copy.start()
            copies.append(copy)
        return copies

    sums = [jnp.sum(m, axis=0, keepdims=True) for m in moments]
    red_layer[layer] = jnp.concatenate(sums + [jnp.zeros((2, 128), jnp.float32)], axis=0)
    first = exchange(layer_peers, layer, lambda d, device: red_layer.at[layer], red_layer, red_ssem.at[0], red_rsem.at[0])
    for copy in first:
        copy.wait_recv()
    red_slab[slab] = sum(red_layer[i] for i in range(n_layer))
    second = exchange(slab_peers, slab, lambda d, device: red_slab.at[slab], red_slab, red_ssem.at[1], red_rsem.at[1])
    for copy in second:
        copy.wait_recv()
    total = jnp.sum(sum(red_slab[i] for i in range(n_slab)), axis=1, keepdims=True)
    scales = [2.0 * c for c in cg_coefficients([total[k : k + 1] for k in range(6)])]

    for j in range(CHUNKS):
        value = scales[0] * here(1, j) + scales[1] * here(2, j) + scales[2] * here(3, j)
        x_buf[:, j * width : (j + 1) * width] = value
        for t in range(width // TILE):
            x_tiles[j * (width // TILE) + t] = value[:, t * TILE : (t + 1) * TILE]
    x_copy = pltpu.make_async_copy(x_buf, x_out.at[0], out_sem)
    x_copy.start()

    lane = lax.broadcasted_iota(jnp.int32, (rows, TILE), 1) // strip

    def pack(owner, carry):
        packed = table[owner]
        pieces = [None] * n_layer
        for q in range(capacity):
            t = lax.shift_right_logical(packed, 8 * (capacity - 1 - q)) & 255
            tile = x_tiles[t]
            for target_layer in range(n_layer):
                shift = ((q - target_layer) * strip) % TILE
                moved = tile if shift == 0 else pltpu.roll(tile, shift, 1)
                old = pieces[target_layer]
                pieces[target_layer] = moved if old is None else jnp.where(lane == q, moved, old)
        for target_layer in range(n_layer):
            strip_send[target_layer, owner] = pieces[target_layer]
        return carry

    lax.fori_loop(0, n_slab, pack, 0)
    third = exchange(
        layer_peers, layer, lambda d, device: strip_send.at[device["layer"]], strip_recv, strip_ssem, strip_rsem
    )
    strip_recv[layer] = strip_send[layer]
    for copy in third:
        copy.wait_recv()
    for owner in range(n_slab):
        tile_send[owner] = sum(strip_recv[i, owner] for i in range(n_layer))
    fourth = exchange(
        slab_peers, slab, lambda d, device: tile_send.at[device["slab"]], tile_recv, tile_ssem, tile_rsem
    )
    tile_recv[slab] = tile_send[slab]
    for copy in fourth:
        copy.wait_recv()
    if tile_rows == 1:
        turned = jnp.transpose(tile_recv[...].reshape(TILE, TILE))
        for k in range(owned_count):
            g_out[k] = turned[k * strip : (k + 1) * strip]
    else:
        count = jnp.int32(0)
        picked = [jnp.int32(0)] * owned_count
        for r in range(tile_rows):
            for t in range(tiles_across):
                mine = owner_ref[r, t] == slab
                picked = [jnp.where(mine & (count == k), r, p) for k, p in enumerate(picked)]
                count = jnp.where(mine, count + 1, count)
        for k in range(owned_count):
            block = tile_recv[pl.ds(picked[k] * per_tile, per_tile)].reshape(TILE, TILE)
            g_out[k] = jnp.transpose(block)[0:strip]

    for stage in range(4):
        for j in range(CHUNKS):
            for direction in range(4):
                if used(stage, direction, j):

                    @pl.when(sends_to[direction])
                    def _():
                        halo_copy(stage, direction, j).wait_send()

    for copy in first + second + third + fourth:
        copy.wait_send()
    x_copy.wait()


def per_device(adjoint_source, conductivity, tile_owner):
    n_slab, n_layer = lax.axis_size("slab"), lax.axis_size("layer")
    depth, rows, cols = adjoint_source.shape
    owned = tile_owner.shape[0] * tile_owner.shape[1] // n_slab
    strip = TILE // n_layer
    width = cols // CHUNKS
    vmem = pl.BlockSpec(memory_space=pltpu.VMEM)
    f32 = jnp.float32
    return pl.pallas_call(
        functools.partial(kernel, n_slab, n_layer),
        out_shape=(
            jax.ShapeDtypeStruct((depth, rows, cols), f32),
            jax.ShapeDtypeStruct((owned, strip, TILE), f32),
        ),
        in_specs=[vmem, vmem, pl.BlockSpec(memory_space=pltpu.SMEM)],
        out_specs=(pl.BlockSpec(memory_space=pl.ANY), vmem),
        scratch_shapes=[
            pltpu.VMEM((4, rows + 16, cols + 2 * PAD), f32),
            pltpu.VMEM((6, rows, cols), f32),
            pltpu.VMEM((rows, cols), f32),
            pltpu.VMEM((4, 2, rows, cols), f32),
            pltpu.VMEM((4, 2, CHUNKS, 1, width), f32),
            pltpu.VMEM((4, 2, CHUNKS, 1, width), f32),
            pltpu.VMEM((n_layer, 8, 128), f32),
            pltpu.VMEM((n_slab, 8, 128), f32),
            pltpu.VMEM((rows, cols), f32),
            pltpu.VMEM((cols // TILE, rows, TILE), f32),
            pltpu.VMEM((n_layer, n_slab, rows, TILE), f32),
            pltpu.VMEM((n_layer, n_slab, rows, TILE), f32),
            pltpu.VMEM((n_slab, rows, TILE), f32),
            pltpu.VMEM((n_slab, rows, TILE), f32),
            pltpu.SMEM((n_slab,), jnp.int32),
            pltpu.SemaphoreType.DMA((4, 4, CHUNKS)),
            pltpu.SemaphoreType.DMA((4, 4, CHUNKS)),
            pltpu.SemaphoreType.DMA((2, max(n_slab, n_layer))),
            pltpu.SemaphoreType.DMA((2, max(n_slab, n_layer))),
            pltpu.SemaphoreType.DMA((n_layer,)),
            pltpu.SemaphoreType.DMA((n_layer,)),
            pltpu.SemaphoreType.DMA((n_slab,)),
            pltpu.SemaphoreType.DMA((n_slab,)),
            pltpu.SemaphoreType.DMA,
        ],
        compiler_params=pltpu.CompilerParams(
            collective_id=0, has_side_effects=True, vmem_limit_bytes=48 * 1024 * 1024
        ),
        name="stack_cg",
    )(adjoint_source, conductivity, tile_owner)


def solution(mesh):
    placed = (P("layer", "slab", None), P("layer", "slab", None), P())
    return jax.shard_map(
        per_device,
        mesh=mesh,
        in_specs=placed,
        out_specs=(P("layer", "slab", None), P("slab", "layer", None)),
        check_vma=False,
    )
```

time: 282 us -> 42.4 us (0.15)
  blocking collectives: 144 us -> 0 us
  waiting for transfers between devices: 47.4 us -> 0 us
  starting transfers between devices: 46.5 us -> 0 us
  Pallas kernels: 0 us -> 37.7 us
  between operations: 21 us -> 0.65 us
  other arithmetic: 14.9 us -> 0 us
    psum x10 -> x0, blocking collectives: 144 us -> none  [the longest x5 93.8 us: combined(): slab_total = lax.psum(value, 'slab')]
    ppermute x16 -> x0, starting transfers between devices: 40.9 us -> none  [the longest x8 30.5 us: padded_2(): lax.ppermute(lax.slice_in_dim(block, block.shape[dim] - width, None, axis...]
    pallas_call x0 -> x1, Pallas kernels: none -> 37.7 us  [per_device(): pl.pallas_call(functools.partial(kernel, n_slab, n_layer), out_shape=(jax...]
    ppermute x16 -> x0, waiting for transfers between devices: 22 us -> none  [the longest x8 16.8 us: padded_2(): lax.ppermute(lax.slice_in_dim(block, 0, width, axis=dim), axis, backward)]
    unnamed x2 -> x0, waiting for transfers between devices: 18.6 us -> none
    reduce_sum x7 -> x0, other arithmetic: 7.05 us -> none  [the longest x3 3.59 us: per_device(): step_size = inner_now / combined(jnp.sum(direction * result))]
    all_to_all x1 -> x0, waiting for transfers between devices: 6.83 us -> none  [per_device(): lax.all_to_all(outgoing, 'slab', split_axis=0, concat_axis=0, tiled=True)]
    all_to_all x1 -> x0, starting transfers between devices: 5.52 us -> none  [per_device(): lax.all_to_all(outgoing, 'slab', split_axis=0, concat_axis=0, tiled=True)]
  transfers between devices with their start and end apart: 18 -> 0, of which waited for: 13 -> 0; matrix products, arithmetic and copies ran while one was open for 0% -> 0% of each run, Pallas kernels for 0% -> 0%
where the time goes in v1:
time: 42.4 us; the launch traced here: 42.2 us
  Pallas kernels  37.7 us (89%)
  local copies, waits for them, and re-layouts  3.88 us (9%)
  between operations  0.65 us (2%)
    pallas_call x1, Pallas kernels, per_device(): pl.pallas_call(functools.partial(kernel, n_slab, n_layer), out_shape=(jax...  37.7 us
    unnamed x8, local copies, waits for them, and re-layouts  3.88 us

profile of v1, /device:TPU:0, one launch (start us, length us, event | category | flops | bytes accessed | tf_op | source)
XLA Modules:
  0.0 42.2 jit_solution(1222815456091116741)
XLA Ops:
  0.6 0.0 copy-start
  0.6 0.9 %copy-done = f32[1,16,4096]{2,1,0:T(8,128)S(1)} copy-done((f32[1,16,4096]{2,1,0:T(8,128)S(1)}, f32[1,16,4096]{2,1,0:T(8,128)}, u32[]{:S(2)}) %copy-start) | copy-done | bytes 262168
  1.6 0.0 copy-start.1
  1.6 0.9 %copy-done.1 = f32[1,16,4096]{2,1,0:T(8,128)S(1)} copy-done((f32[1,16,4096]{2,1,0:T(8,128)S(1)}, f32[1,16,4096]{2,1,0:T(8,128)}, u32[]{:S(2)}) %copy-start.1) | copy-done | bytes 262168
  2.5 0.0 copy-start.2
  2.5 0.7 %copy-done.2 = s32[1,32]{1,0:T(1,128)S(1)} copy-done((s32[1,32]{1,0:T(1,128)S(1)}, s32[1,32]{1,0:T(1,128)}, u32[]{:S(2)}) %copy-start.2) | copy-done | bytes 152
  3.2 37.7 %stack_cg.1 = (f32[1,16,4096]{2,1,0:T(8,128)S(1)}, f32[4,32,128]{2,1,0:T(8,128)S(1)}) custom-call(f32[1,16,4096]{2,1,0:T(8,128)S(1)} %copy-done, f32[1,16,4096]{2,1,0:T(8,128)S(1)} %copy-done.1, s32[1,32]{1,0:T(1,128)S(1)} %copy-done.2), custom_call_target="tpu_custom_call" | custom-call | tf_op jit(solution)/shard_map/stack_cg/pallas_call | solution.py:376
  40.9 0.7 %copy.7 = f32[1,16,4096]{2,1,0:T(8,128)} copy(f32[1,16,4096]{2,1,0:T(8,128)S(1)} %get-tuple-element.4) | data formatting | bytes 524288
  41.6 0.6 %copy.8 = f32[4,32,128]{2,1,0:T(8,128)} copy(f32[4,32,128]{2,1,0:T(8,128)S(1)} %get-tuple-element.5) | data formatting | bytes 131072
Async XLA Ops:
  0.6 1.0 %copy-start = (f32[1,16,4096]{2,1,0:T(8,128)S(1)}, f32[1,16,4096]{2,1,0:T(8,128)}, u32[]{:S(2)}) copy-start(f32[1,16,4096]{2,1,0:T(8,128)} %src_ref.1) | copy-start | bytes 786436
  1.6 0.9 %copy-start.1 = (f32[1,16,4096]{2,1,0:T(8,128)S(1)}, f32[1,16,4096]{2,1,0:T(8,128)}, u32[]{:S(2)}) copy-start(f32[1,16,4096]{2,1,0:T(8,128)} %cond_ref.1) | copy-start | bytes 786436
  2.5 0.7 %copy-start.2 = (s32[1,32]{1,0:T(1,128)S(1)}, s32[1,32]{1,0:T(1,128)}, u32[]{:S(2)}) copy-start(s32[1,32]{1,0:T(1,128)} %owner_ref.1) | copy-start | bytes 388

commit v2 on v1

--- a/solution.py
+++ b/solution.py
@@ -60,11 +60,13 @@
 def kernel(
     n_slab,
     n_layer,
-    src_ref,
-    cond_ref,
-    owner_ref,
+    src_hbm,
+    cond_hbm,
+    owner_hbm,
     x_out,
     g_out,
+    src_ref,
+    owner_ref,
     fields,
     coefs,
     inv_ref,
@@ -75,8 +77,6 @@
     red_slab,
     x_buf,
     x_tiles,
-    strip_send,
-    strip_recv,
     tile_send,
     tile_recv,
     table,
@@ -84,15 +84,13 @@
     halo_rsem,
     red_ssem,
     red_rsem,
-    strip_ssem,
-    strip_rsem,
     tile_ssem,
     tile_rsem,
-    out_sem,
+    local_sem,
 ):
     slab = lax.axis_index("slab")
     layer = lax.axis_index("layer")
-    rows, cols = src_ref.shape[1], src_ref.shape[2]
+    rows, cols = src_ref.shape
     width = cols // CHUNKS
     top, bottom = 8, 8 + rows
     tile_rows, tiles_across = owner_ref.shape
@@ -101,15 +99,50 @@
     owned_count = g_out.shape[0]
     per_tile = TILE // rows
 
-    def peers(axis, me, count):
-        return [(d, {axis: lax.rem(me + d, count)}, lax.rem(me + count - d, count)) for d in range(1, count)]
-
-    layer_peers = peers("layer", layer, n_layer)
-    slab_peers = peers("slab", slab, n_slab)
+    pair, core = layer // 2, layer % 2
+    n_pair = n_layer // 2
+
+    def turn(me, d, count):
+        return lax.rem(me + d, count)
+
+    def layer_peer(d):
+        return {"layer": turn(layer, d, n_layer)}
+
+    def slab_peer(d):
+        return {"slab": turn(slab, d, n_slab)}
+
+    def tile_peer(n):
+        to_pair, to_slab = turn(pair, n // n_slab, n_pair), turn(slab, n % n_slab, n_slab)
+        return to_pair, to_slab, {"layer": 2 * to_pair + core, "slab": to_slab}
+
+    def repeat(start, stop, body):
+        if stop - start <= 32:
+            for n in range(start, stop):
+                body(n)
+        else:
+            lax.fori_loop(start, stop, lambda n, carry: (body(n), carry)[1], 0)
 
     barrier = pltpu.get_barrier_semaphore()
-    for _, device, _ in layer_peers + slab_peers:
+
+    def greet(device):
         pl.semaphore_signal(barrier, inc=1, device_id=device, device_id_type=MESH)
+
+    n_greet = 0
+    for d in range(1, n_layer):
+        if d % 2 == 1:
+            greet(layer_peer(d))
+            n_greet += 1
+    repeat(1, n_pair * n_slab, lambda n: greet(tile_peer(n)[2]))
+    n_greet += n_pair * n_slab - 1
+
+    cond_copy = pltpu.make_async_copy(
+        cond_hbm.at[0], fields.at[0, pl.ds(top, rows), pl.ds(PAD, cols)], local_sem.at[0]
+    )
+    src_copy = pltpu.make_async_copy(src_hbm.at[0], src_ref, local_sem.at[1])
+    owner_copy = pltpu.make_async_copy(owner_hbm, owner_ref, local_sem.at[2])
+    cond_copy.start()
+    src_copy.start()
+    owner_copy.start()
 
     for s in range(4):
         fields[s, :, 0:PAD] = jnp.zeros((rows + 16, PAD), jnp.float32)
@@ -141,11 +174,14 @@
     def used(stage, direction, j):
         if stage < 3:
             return True
-        if direction == 0:
-            return j < CHUNKS // 2
-        if direction == 1:
-            return j >= CHUNKS // 2
-        return direction == 2
+        return direction < 3
+
+    def wanted(stage, direction, j, sender_layer):
+        if stage == 3 and direction == 0 and j >= CHUNKS // 2:
+            return sender_layer % 2 == 0
+        if stage == 3 and direction == 1 and j < CHUNKS // 2:
+            return sender_layer % 2 == 1
+        return True
 
     def halo_copy(stage, direction, j):
         span = pl.ds(j * width, width)
@@ -173,7 +209,7 @@
         for direction in range(4):
             if used(stage, direction, j):
 
-                @pl.when(sends_to[direction])
+                @pl.when(sends_to[direction] & wanted(stage, direction, j, layer))
                 def _():
                     halo_copy(stage, direction, j).start()
 
@@ -181,7 +217,7 @@
         for direction in range(4):
             if used(stage, direction, j):
 
-                @pl.when(gets_from[direction])
+                @pl.when(gets_from[direction] & wanted(stage, direction, j, layer + 1))
                 def _():
                     halo_copy(stage, direction, j).wait_recv()
 
@@ -210,12 +246,15 @@
     def here(stage, j):
         return fields[stage, top:bottom, PAD + j * width : PAD + (j + 1) * width]
 
-    for j in range(CHUNKS):
-        put_field(0, j, cond_ref[0, :, j * width : (j + 1) * width])
-    pl.semaphore_wait(barrier, n_layer + n_slab - 2)
+    cond_copy.wait()
+    for j in range(CHUNKS):
+        row_send[0, 0, j] = fields[0, bottom - 1 : bottom, PAD + j * width : PAD + (j + 1) * width]
+        row_send[0, 1, j] = fields[0, top : top + 1, PAD + j * width : PAD + (j + 1) * width]
+    pl.semaphore_wait(barrier, n_greet)
     for j in range(CHUNKS):
         send_field(0, j)
 
+    owner_copy.wait()
     my_row = slab // per_tile
 
     def list_tiles(owner, carry):
@@ -227,6 +266,7 @@
 
     lax.fori_loop(0, n_slab, list_tiles, 0)
 
+    src_copy.wait()
     moments = [jnp.zeros((8, 128), jnp.float32) for _ in range(6)]
     for j in range(CHUNKS):
         get_halo(0, j)
@@ -239,7 +279,7 @@
             diagonal = face if diagonal is None else diagonal + face
         inverse = 1.0 / diagonal
         inv_ref[:, span] = inverse
-        source = src_ref[0, :, span]
+        source = src_ref[:, span]
         field = source * inverse
         put_field(1, j, field)
         send_field(1, j)
@@ -268,75 +308,88 @@
         moments[5] = moments[5] + fold(here(3, j) * image)
     moments[5] = 2.0 * moments[5]
 
-    def exchange(peer_list, me, send_of, recv_buf, ssem, rsem):
-        copies = []
-        for d, device, _ in peer_list:
-            copy = pltpu.make_async_remote_copy(
-                src_ref=send_of(d, device),
-                dst_ref=recv_buf.at[me],
-                send_sem=ssem.at[d],
-                recv_sem=rsem.at[d],
-                device_id=device,
-                device_id_type=MESH,
-            )
-            copy.start()
-            copies.append(copy)
-        return copies
+    def layer_sum_copy(d):
+        return pltpu.make_async_remote_copy(
+            src_ref=red_layer.at[layer],
+            dst_ref=red_layer.at[layer],
+            send_sem=red_ssem.at[0, d],
+            recv_sem=red_rsem.at[0, d],
+            device_id=layer_peer(d),
+            device_id_type=MESH,
+        )
+
+    def slab_sum_copy(d):
+        return pltpu.make_async_remote_copy(
+            src_ref=red_slab.at[slab],
+            dst_ref=red_slab.at[slab],
+            send_sem=red_ssem.at[1, d],
+            recv_sem=red_rsem.at[1, d],
+            device_id=slab_peer(d),
+            device_id_type=MESH,
+        )
+
+    def tile_copy(n):
+        to_pair, to_slab, device = tile_peer(n)
+        return pltpu.make_async_remote_copy(
+            src_ref=tile_send.at[to_pair, to_slab],
+            dst_ref=tile_recv.at[pair, slab],
+            send_sem=tile_ssem.at[n],
+            recv_sem=tile_rsem.at[n],
+            device_id=device,
+            device_id_type=MESH,
+        )
 
     sums = [jnp.sum(m, axis=0, keepdims=True) for m in moments]
     red_layer[layer] = jnp.concatenate(sums + [jnp.zeros((2, 128), jnp.float32)], axis=0)
-    first = exchange(layer_peers, layer, lambda d, device: red_layer.at[layer], red_layer, red_ssem.at[0], red_rsem.at[0])
-    for copy in first:
-        copy.wait_recv()
+    repeat(1, n_layer, lambda d: layer_sum_copy(d).start())
+    repeat(1, n_layer, lambda d: layer_sum_copy(d).wait_recv())
     red_slab[slab] = sum(red_layer[i] for i in range(n_layer))
-    second = exchange(slab_peers, slab, lambda d, device: red_slab.at[slab], red_slab, red_ssem.at[1], red_rsem.at[1])
-    for copy in second:
-        copy.wait_recv()
+    repeat(1, n_slab, lambda d: slab_sum_copy(d).start())
+    repeat(1, n_slab, lambda d: slab_sum_copy(d).wait_recv())
     total = jnp.sum(sum(red_slab[i] for i in range(n_slab)), axis=1, keepdims=True)
     scales = [2.0 * c for c in cg_coefficients([total[k : k + 1] for k in range(6)])]
 
     for j in range(CHUNKS):
-        value = scales[0] * here(1, j) + scales[1] * here(2, j) + scales[2] * here(3, j)
-        x_buf[:, j * width : (j + 1) * width] = value
+        value = None
+        for k in range(ITERS):
+            near_field = layer_halo[k + 1, 1 - core, :, j * width : (j + 1) * width]
+            term = scales[k] * (here(k + 1, j) + near_field)
+            value = term if value is None else value + term
         for t in range(width // TILE):
             x_tiles[j * (width // TILE) + t] = value[:, t * TILE : (t + 1) * TILE]
-    x_copy = pltpu.make_async_copy(x_buf, x_out.at[0], out_sem)
-    x_copy.start()
 
     lane = lax.broadcasted_iota(jnp.int32, (rows, TILE), 1) // strip
 
     def pack(owner, carry):
         packed = table[owner]
-        pieces = [None] * n_layer
+        pieces = [None] * n_pair
         for q in range(capacity):
             t = lax.shift_right_logical(packed, 8 * (capacity - 1 - q)) & 255
             tile = x_tiles[t]
-            for target_layer in range(n_layer):
-                shift = ((q - target_layer) * strip) % TILE
+            tile = jnp.where(core == 1, pltpu.roll(tile, TILE - strip, 1), tile)
+            for p in range(n_pair):
+                shift = ((q - 2 * p) * strip) % TILE
                 moved = tile if shift == 0 else pltpu.roll(tile, shift, 1)
-                old = pieces[target_layer]
-                pieces[target_layer] = moved if old is None else jnp.where(lane == q, moved, old)
-        for target_layer in range(n_layer):
-            strip_send[target_layer, owner] = pieces[target_layer]
+                pieces[p] = moved if q == 0 else jnp.where(lane == q, moved, pieces[p])
+        for p in range(n_pair):
+            tile_send[p, owner] = pieces[p]
         return carry
 
     lax.fori_loop(0, n_slab, pack, 0)
-    third = exchange(
-        layer_peers, layer, lambda d, device: strip_send.at[device["layer"]], strip_recv, strip_ssem, strip_rsem
-    )
-    strip_recv[layer] = strip_send[layer]
-    for copy in third:
-        copy.wait_recv()
-    for owner in range(n_slab):
-        tile_send[owner] = sum(strip_recv[i, owner] for i in range(n_layer))
-    fourth = exchange(
-        slab_peers, slab, lambda d, device: tile_send.at[device["slab"]], tile_recv, tile_ssem, tile_rsem
-    )
-    tile_recv[slab] = tile_send[slab]
-    for copy in fourth:
-        copy.wait_recv()
+    repeat(1, n_pair * n_slab, lambda n: tile_copy(n).start())
+
+    for j in range(CHUNKS):
+        value = scales[0] * here(1, j) + scales[1] * here(2, j) + scales[2] * here(3, j)
+        x_buf[:, j * width : (j + 1) * width] = value
+    x_copy = pltpu.make_async_copy(x_buf, x_out.at[0], local_sem.at[0])
+    x_copy.start()
+
+    tile_recv[pair, slab] = tile_send[pair, slab]
+    repeat(1, n_pair * n_slab, lambda n: tile_copy(n).wait_recv())
+    for i in range(n_slab):
+        tile_recv[0, i] = sum(tile_recv[p, i] for p in range(n_pair))
     if tile_rows == 1:
-        turned = jnp.transpose(tile_recv[...].reshape(TILE, TILE))
+        turned = jnp.transpose(tile_recv[0].reshape(TILE, TILE))
         for k in range(owned_count):
             g_out[k] = turned[k * strip : (k + 1) * strip]
     else:
@@ -348,7 +401,7 @@
                 picked = [jnp.where(mine & (count == k), r, p) for k, p in enumerate(picked)]
                 count = jnp.where(mine, count + 1, count)
         for k in range(owned_count):
-            block = tile_recv[pl.ds(picked[k] * per_tile, per_tile)].reshape(TILE, TILE)
+            block = tile_recv[0, pl.ds(picked[k] * per_tile, per_tile)].reshape(TILE, TILE)
             g_out[k] = jnp.transpose(block)[0:strip]
 
     for stage in range(4):
@@ -356,12 +409,13 @@
             for direction in range(4):
                 if used(stage, direction, j):
 
-                    @pl.when(sends_to[direction])
+                    @pl.when(sends_to[direction] & wanted(stage, direction, j, layer))
                     def _():
                         halo_copy(stage, direction, j).wait_send()
 
-    for copy in first + second + third + fourth:
-        copy.wait_send()
+    repeat(1, n_layer, lambda d: layer_sum_copy(d).wait_send())
+    repeat(1, n_slab, lambda d: slab_sum_copy(d).wait_send())
+    repeat(1, n_pair * n_slab, lambda n: tile_copy(n).wait_send())
     x_copy.wait()
 
 
@@ -379,9 +433,11 @@
             jax.ShapeDtypeStruct((depth, rows, cols), f32),
             jax.ShapeDtypeStruct((owned, strip, TILE), f32),
         ),
-        in_specs=[vmem, vmem, pl.BlockSpec(memory_space=pltpu.SMEM)],
+        in_specs=[pl.BlockSpec(memory_space=pl.ANY)] * 3,
         out_specs=(pl.BlockSpec(memory_space=pl.ANY), vmem),
         scratch_shapes=[
+            pltpu.VMEM((rows, cols), f32),
+            pltpu.SMEM(tile_owner.shape, jnp.int32),
             pltpu.VMEM((4, rows + 16, cols + 2 * PAD), f32),
             pltpu.VMEM((6, rows, cols), f32),
             pltpu.VMEM((rows, cols), f32),
@@ -392,20 +448,16 @@
             pltpu.VMEM((n_slab, 8, 128), f32),
             pltpu.VMEM((rows, cols), f32),
             pltpu.VMEM((cols // TILE, rows, TILE), f32),
-            pltpu.VMEM((n_layer, n_slab, rows, TILE), f32),
-            pltpu.VMEM((n_layer, n_slab, rows, TILE), f32),
-            pltpu.VMEM((n_slab, rows, TILE), f32),
-            pltpu.VMEM((n_slab, rows, TILE), f32),
+            pltpu.VMEM((n_layer // 2, n_slab, rows, TILE), f32),
+            pltpu.VMEM((n_layer // 2, n_slab, rows, TILE), f32),
             pltpu.SMEM((n_slab,), jnp.int32),
             pltpu.SemaphoreType.DMA((4, 4, CHUNKS)),
             pltpu.SemaphoreType.DMA((4, 4, CHUNKS)),
             pltpu.SemaphoreType.DMA((2, max(n_slab, n_layer))),
             pltpu.SemaphoreType.DMA((2, max(n_slab, n_layer))),
-            pltpu.SemaphoreType.DMA((n_layer,)),
-            pltpu.SemaphoreType.DMA((n_layer,)),
-            pltpu.SemaphoreType.DMA((n_slab,)),
-            pltpu.SemaphoreType.DMA((n_slab,)),
-            pltpu.SemaphoreType.DMA,
+            pltpu.SemaphoreType.DMA((n_layer // 2 * n_slab,)),
+            pltpu.SemaphoreType.DMA((n_layer // 2 * n_slab,)),
+            pltpu.SemaphoreType.DMA((3,)),
         ],
         compiler_params=pltpu.CompilerParams(
             collective_id=0, has_side_effects=True, vmem_limit_bytes=48 * 1024 * 1024

time: 42.4 us -> 40 us (0.943)
  Pallas kernels: 37.7 us -> 35.3 us
    pallas_call x1, Pallas kernels: 37.7 us -> 35.3 us  [per_device(): pl.pallas_call(functools.partial(kernel, n_slab, n_layer), out_shape=(jax...]
where the time goes in v2:
time: 40 us; the launch traced here: 39.8 us
  Pallas kernels  35.3 us (88%)
  local copies, waits for them, and re-layouts  3.88 us (10%)
  between operations  0.65 us (2%)
    pallas_call x1, Pallas kernels, per_device(): pl.pallas_call(functools.partial(kernel, n_slab, n_layer), out_shape=(jax...  35.3 us
    unnamed x8, local copies, waits for them, and re-layouts  3.88 us

profile of v2, /device:TPU:0, one launch (start us, length us, event | category | flops | bytes accessed | tf_op | source)
XLA Modules:
  0.0 39.8 jit_solution(5587431007004069138)
XLA Ops:
  0.6 0.0 copy-start
  0.6 0.9 %copy-done = f32[1,16,4096]{2,1,0:T(8,128)S(1)} copy-done((f32[1,16,4096]{2,1,0:T(8,128)S(1)}, f32[1,16,4096]{2,1,0:T(8,128)}, u32[]{:S(2)}) %copy-start) | copy-done | bytes 262168
  1.6 0.0 copy-start.1
  1.6 0.9 %copy-done.1 = f32[1,16,4096]{2,1,0:T(8,128)S(1)} copy-done((f32[1,16,4096]{2,1,0:T(8,128)S(1)}, f32[1,16,4096]{2,1,0:T(8,128)}, u32[]{:S(2)}) %copy-start.1) | copy-done | bytes 262168
  2.5 0.0 copy-start.2
  2.5 0.7 %copy-done.2 = s32[1,32]{1,0:T(1,128)S(1)} copy-done((s32[1,32]{1,0:T(1,128)S(1)}, s32[1,32]{1,0:T(1,128)}, u32[]{:S(2)}) %copy-start.2) | copy-done | bytes 152
  3.2 35.3 %stack_cg.1 = (f32[1,16,4096]{2,1,0:T(8,128)S(1)}, f32[4,32,128]{2,1,0:T(8,128)S(1)}) custom-call(f32[1,16,4096]{2,1,0:T(8,128)S(1)} %copy-done, f32[1,16,4096]{2,1,0:T(8,128)S(1)} %copy-done.1, s32[1,32]{1,0:T(1,128)S(1)} %copy-done.2), custom_call_target="tpu_custom_call" | custom-call | tf_op jit(solution)/shard_map/stack_cg/pallas_call | solution.py:430
  38.5 0.7 %copy.7 = f32[1,16,4096]{2,1,0:T(8,128)} copy(f32[1,16,4096]{2,1,0:T(8,128)S(1)} %get-tuple-element.4) | data formatting | bytes 524288
  39.2 0.6 %copy.8 = f32[4,32,128]{2,1,0:T(8,128)} copy(f32[4,32,128]{2,1,0:T(8,128)S(1)} %get-tuple-element.5) | data formatting | bytes 131072
Async XLA Ops:
  0.6 1.0 %copy-start = (f32[1,16,4096]{2,1,0:T(8,128)S(1)}, f32[1,16,4096]{2,1,0:T(8,128)}, u32[]{:S(2)}) copy-start(f32[1,16,4096]{2,1,0:T(8,128)} %src_hbm.1) | copy-start | bytes 786436
  1.6 0.9 %copy-start.1 = (f32[1,16,4096]{2,1,0:T(8,128)S(1)}, f32[1,16,4096]{2,1,0:T(8,128)}, u32[]{:S(2)}) copy-start(f32[1,16,4096]{2,1,0:T(8,128)} %cond_hbm.1) | copy-start | bytes 786436
  2.5 0.7 %copy-start.2 = (s32[1,32]{1,0:T(1,128)S(1)}, s32[1,32]{1,0:T(1,128)}, u32[]{:S(2)}) copy-start(s32[1,32]{1,0:T(1,128)} %owner_hbm.1) | copy-start | bytes 388

commit v3 on v2

--- a/solution.py
+++ b/solution.py
@@ -9,7 +9,7 @@
 
 TILE = 128
 ITERS = 3
-CHUNKS = 4
+CHUNKS = 2
 PAD = 128
 MESH = pl.DeviceIdType.MESH
 
@@ -433,7 +433,7 @@
             jax.ShapeDtypeStruct((depth, rows, cols), f32),
             jax.ShapeDtypeStruct((owned, strip, TILE), f32),
         ),
-        in_specs=[pl.BlockSpec(memory_space=pl.ANY)] * 3,
+        in_specs=[pl.BlockSpec(memory_space=pltpu.HBM)] * 3,
         out_specs=(pl.BlockSpec(memory_space=pl.ANY), vmem),
         scratch_shapes=[
             pltpu.VMEM((rows, cols), f32),

time: 40 us -> 41.4 us (1.035)
  Pallas kernels: 35.3 us -> 36.7 us
    pallas_call x1, Pallas kernels: 35.3 us -> 36.7 us  [per_device(): pl.pallas_call(functools.partial(kernel, n_slab, n_layer), out_shape=(jax...]
where the time goes in v3:
time: 41.4 us; the launch traced here: 41.2 us
  Pallas kernels  36.7 us (89%)
  local copies, waits for them, and re-layouts  3.88 us (9%)
  between operations  0.65 us (2%)
    pallas_call x1, Pallas kernels, per_device(): pl.pallas_call(functools.partial(kernel, n_slab, n_layer), out_shape=(jax...  36.7 us
    unnamed x8, local copies, waits for them, and re-layouts  3.88 us

profile of v3, /device:TPU:0, one launch (start us, length us, event | category | flops | bytes accessed | tf_op | source)
XLA Modules:
  0.0 41.2 jit_solution(16933317502937131652)
XLA Ops:
  0.6 0.0 copy-start
  0.6 0.9 %copy-done = f32[1,16,4096]{2,1,0:T(8,128)S(1)} copy-done((f32[1,16,4096]{2,1,0:T(8,128)S(1)}, f32[1,16,4096]{2,1,0:T(8,128)}, u32[]{:S(2)}) %copy-start) | copy-done | bytes 262168
  1.6 0.0 copy-start.1
  1.6 0.9 %copy-done.1 = f32[1,16,4096]{2,1,0:T(8,128)S(1)} copy-done((f32[1,16,4096]{2,1,0:T(8,128)S(1)}, f32[1,16,4096]{2,1,0:T(8,128)}, u32[]{:S(2)}) %copy-start.1) | copy-done | bytes 262168
  2.5 0.0 copy-start.2
  2.5 0.7 %copy-done.2 = s32[1,32]{1,0:T(1,128)S(1)} copy-done((s32[1,32]{1,0:T(1,128)S(1)}, s32[1,32]{1,0:T(1,128)}, u32[]{:S(2)}) %copy-start.2) | copy-done | bytes 152
  3.2 36.7 %stack_cg.1 = (f32[1,16,4096]{2,1,0:T(8,128)S(1)}, f32[4,32,128]{2,1,0:T(8,128)S(1)}) custom-call(f32[1,16,4096]{2,1,0:T(8,128)S(1)} %copy-done, f32[1,16,4096]{2,1,0:T(8,128)S(1)} %copy-done.1, s32[1,32]{1,0:T(1,128)S(1)} %copy-done.2), custom_call_target="tpu_custom_call" | custom-call | tf_op jit(solution)/shard_map/stack_cg/pallas_call | solution.py:430
  39.9 0.7 %copy.7 = f32[1,16,4096]{2,1,0:T(8,128)} copy(f32[1,16,4096]{2,1,0:T(8,128)S(1)} %get-tuple-element.4) | data formatting | bytes 524288
  40.6 0.6 %copy.8 = f32[4,32,128]{2,1,0:T(8,128)} copy(f32[4,32,128]{2,1,0:T(8,128)S(1)} %get-tuple-element.5) | data formatting | bytes 131072
Async XLA Ops:
  0.6 1.0 %copy-start = (f32[1,16,4096]{2,1,0:T(8,128)S(1)}, f32[1,16,4096]{2,1,0:T(8,128)}, u32[]{:S(2)}) copy-start(f32[1,16,4096]{2,1,0:T(8,128)} %src_hbm.1) | copy-start | bytes 786436
  1.6 0.9 %copy-start.1 = (f32[1,16,4096]{2,1,0:T(8,128)S(1)}, f32[1,16,4096]{2,1,0:T(8,128)}, u32[]{:S(2)}) copy-start(f32[1,16,4096]{2,1,0:T(8,128)} %cond_hbm.1) | copy-start | bytes 786436
  2.5 0.7 %copy-start.2 = (s32[1,32]{1,0:T(1,128)S(1)}, s32[1,32]{1,0:T(1,128)}, u32[]{:S(2)}) copy-start(s32[1,32]{1,0:T(1,128)} %owner_hbm.1) | copy-start | bytes 388

commit v4 on v3

--- a/solution.py
+++ b/solution.py
@@ -9,7 +9,7 @@
 
 TILE = 128
 ITERS = 3
-CHUNKS = 2
+CHUNKS = 4
 PAD = 128
 MESH = pl.DeviceIdType.MESH
 
@@ -79,6 +79,8 @@
     x_tiles,
     tile_send,
     tile_recv,
+    tiles,
+    g_buf,
     table,
     halo_ssem,
     halo_rsem,
@@ -265,6 +267,64 @@
         return carry
 
     lax.fori_loop(0, n_slab, list_tiles, 0)
+
+    def layer_sum_copy(d):
+        return pltpu.make_async_remote_copy(
+            src_ref=red_layer.at[layer],
+            dst_ref=red_layer.at[layer],
+            send_sem=red_ssem.at[0, d],
+            recv_sem=red_rsem.at[0, d],
+            device_id=layer_peer(d),
+            device_id_type=MESH,
+        )
+
+    def slab_sum_copy(d):
+        return pltpu.make_async_remote_copy(
+            src_ref=red_slab.at[slab],
+            dst_ref=red_slab.at[slab],
+            send_sem=red_ssem.at[1, d],
+            recv_sem=red_rsem.at[1, d],
+            device_id=slab_peer(d),
+            device_id_type=MESH,
+        )
+
+    def tile_copy(k, n):
+        to_pair, to_slab, device = tile_peer(n)
+        return pltpu.make_async_remote_copy(
+            src_ref=tile_send.at[k, to_pair, to_slab],
+            dst_ref=tile_recv.at[k, pair, slab],
+            send_sem=tile_ssem.at[k, n],
+            recv_sem=tile_rsem.at[k, n],
+            device_id=device,
+            device_id_type=MESH,
+        )
+
+    lane = lax.broadcasted_iota(jnp.int32, (rows, TILE), 1) // strip
+
+    def deliver(k):
+        for j in range(CHUNKS):
+            value = here(k + 1, j) + layer_halo[k + 1, 1 - core, :, j * width : (j + 1) * width]
+            for t in range(width // TILE):
+                x_tiles[j * (width // TILE) + t] = value[:, t * TILE : (t + 1) * TILE]
+
+        def pack(owner, carry):
+            packed = table[owner]
+            pieces = [None] * n_pair
+            for q in range(capacity):
+                t = lax.shift_right_logical(packed, 8 * (capacity - 1 - q)) & 255
+                tile = x_tiles[t]
+                tile = jnp.where(core == 1, pltpu.roll(tile, TILE - strip, 1), tile)
+                for p in range(n_pair):
+                    shift = ((q - 2 * p) * strip) % TILE
+                    moved = tile if shift == 0 else pltpu.roll(tile, shift, 1)
+                    pieces[p] = moved if q == 0 else jnp.where(lane == q, moved, pieces[p])
+            for p in range(n_pair):
+                tile_send[k, p, owner] = pieces[p]
+            return carry
+
+        lax.fori_loop(0, n_slab, pack, 0)
+        repeat(1, n_pair * n_slab, lambda n: tile_copy(k, n).start())
+        tile_recv[k, pair, slab] = tile_send[k, pair, slab]
 
     src_copy.wait()
     moments = [jnp.zeros((8, 128), jnp.float32) for _ in range(6)]
@@ -297,6 +357,7 @@
             send_field(stage + 1, j)
             moments[2 * stage - 1] = moments[2 * stage - 1] + fold(here(stage, j) * image)
             moments[2 * stage] = moments[2 * stage] + fold(field * image)
+        deliver(stage - 1)
     for j in range(CHUNKS):
         get_halo(3, j)
         span = slice(j * width, (j + 1) * width)
@@ -308,40 +369,10 @@
         moments[5] = moments[5] + fold(here(3, j) * image)
     moments[5] = 2.0 * moments[5]
 
-    def layer_sum_copy(d):
-        return pltpu.make_async_remote_copy(
-            src_ref=red_layer.at[layer],
-            dst_ref=red_layer.at[layer],
-            send_sem=red_ssem.at[0, d],
-            recv_sem=red_rsem.at[0, d],
-            device_id=layer_peer(d),
-            device_id_type=MESH,
-        )
-
-    def slab_sum_copy(d):
-        return pltpu.make_async_remote_copy(
-            src_ref=red_slab.at[slab],
-            dst_ref=red_slab.at[slab],
-            send_sem=red_ssem.at[1, d],
-            recv_sem=red_rsem.at[1, d],
-            device_id=slab_peer(d),
-            device_id_type=MESH,
-        )
-
-    def tile_copy(n):
-        to_pair, to_slab, device = tile_peer(n)
-        return pltpu.make_async_remote_copy(
-            src_ref=tile_send.at[to_pair, to_slab],
-            dst_ref=tile_recv.at[pair, slab],
-            send_sem=tile_ssem.at[n],
-            recv_sem=tile_rsem.at[n],
-            device_id=device,
-            device_id_type=MESH,
-        )
-
     sums = [jnp.sum(m, axis=0, keepdims=True) for m in moments]
     red_layer[layer] = jnp.concatenate(sums + [jnp.zeros((2, 128), jnp.float32)], axis=0)
     repeat(1, n_layer, lambda d: layer_sum_copy(d).start())
+    deliver(2)
     repeat(1, n_layer, lambda d: layer_sum_copy(d).wait_recv())
     red_slab[slab] = sum(red_layer[i] for i in range(n_layer))
     repeat(1, n_slab, lambda d: slab_sum_copy(d).start())
@@ -350,48 +381,27 @@
     scales = [2.0 * c for c in cg_coefficients([total[k : k + 1] for k in range(6)])]
 
     for j in range(CHUNKS):
-        value = None
-        for k in range(ITERS):
-            near_field = layer_halo[k + 1, 1 - core, :, j * width : (j + 1) * width]
-            term = scales[k] * (here(k + 1, j) + near_field)
-            value = term if value is None else value + term
-        for t in range(width // TILE):
-            x_tiles[j * (width // TILE) + t] = value[:, t * TILE : (t + 1) * TILE]
-
-    lane = lax.broadcasted_iota(jnp.int32, (rows, TILE), 1) // strip
-
-    def pack(owner, carry):
-        packed = table[owner]
-        pieces = [None] * n_pair
-        for q in range(capacity):
-            t = lax.shift_right_logical(packed, 8 * (capacity - 1 - q)) & 255
-            tile = x_tiles[t]
-            tile = jnp.where(core == 1, pltpu.roll(tile, TILE - strip, 1), tile)
-            for p in range(n_pair):
-                shift = ((q - 2 * p) * strip) % TILE
-                moved = tile if shift == 0 else pltpu.roll(tile, shift, 1)
-                pieces[p] = moved if q == 0 else jnp.where(lane == q, moved, pieces[p])
-        for p in range(n_pair):
-            tile_send[p, owner] = pieces[p]
-        return carry
-
-    lax.fori_loop(0, n_slab, pack, 0)
-    repeat(1, n_pair * n_slab, lambda n: tile_copy(n).start())
-
-    for j in range(CHUNKS):
         value = scales[0] * here(1, j) + scales[1] * here(2, j) + scales[2] * here(3, j)
         x_buf[:, j * width : (j + 1) * width] = value
     x_copy = pltpu.make_async_copy(x_buf, x_out.at[0], local_sem.at[0])
     x_copy.start()
 
-    tile_recv[pair, slab] = tile_send[pair, slab]
-    repeat(1, n_pair * n_slab, lambda n: tile_copy(n).wait_recv())
-    for i in range(n_slab):
-        tile_recv[0, i] = sum(tile_recv[p, i] for p in range(n_pair))
+    for k in range(ITERS):
+        repeat(1, n_pair * n_slab, lambda n: tile_copy(k, n).wait_recv())
+
+    def combine(i, carry):
+        value = None
+        for k in range(ITERS):
+            term = scales[k] * sum(tile_recv[k, p, i] for p in range(n_pair))
+            value = term if value is None else value + term
+        tiles[i] = value
+        return carry
+
+    lax.fori_loop(0, n_slab, combine, 0)
     if tile_rows == 1:
-        turned = jnp.transpose(tile_recv[0].reshape(TILE, TILE))
+        turned = jnp.transpose(tiles[...].reshape(TILE, TILE))
         for k in range(owned_count):
-            g_out[k] = turned[k * strip : (k + 1) * strip]
+            g_buf[k] = turned[k * strip : (k + 1) * strip]
     else:
         count = jnp.int32(0)
         picked = [jnp.int32(0)] * owned_count
@@ -401,8 +411,11 @@
                 picked = [jnp.where(mine & (count == k), r, p) for k, p in enumerate(picked)]
                 count = jnp.where(mine, count + 1, count)
         for k in range(owned_count):
-            block = tile_recv[0, pl.ds(picked[k] * per_tile, per_tile)].reshape(TILE, TILE)
-            g_out[k] = jnp.transpose(block)[0:strip]
+            block = tiles[pl.ds(picked[k] * per_tile, per_tile)].reshape(TILE, TILE)
+            g_buf[k] = jnp.transpose(block)[0:strip]
+
+    g_copy = pltpu.make_async_copy(g_buf, g_out, local_sem.at[1])
+    g_copy.start()
 
     for stage in range(4):
         for j in range(CHUNKS):
@@ -415,8 +428,10 @@
 
     repeat(1, n_layer, lambda d: layer_sum_copy(d).wait_send())
     repeat(1, n_slab, lambda d: slab_sum_copy(d).wait_send())
-    repeat(1, n_pair * n_slab, lambda n: tile_copy(n).wait_send())
+    for k in range(ITERS):
+        repeat(1, n_pair * n_slab, lambda n: tile_copy(k, n).wait_send())
     x_copy.wait()
+    g_copy.wait()
 
 
 def per_device(adjoint_source, conductivity, tile_owner):
@@ -425,7 +440,6 @@
     owned = tile_owner.shape[0] * tile_owner.shape[1] // n_slab
     strip = TILE // n_layer
     width = cols // CHUNKS
-    vmem = pl.BlockSpec(memory_space=pltpu.VMEM)
     f32 = jnp.float32
     return pl.pallas_call(
         functools.partial(kernel, n_slab, n_layer),
@@ -434,7 +448,7 @@
             jax.ShapeDtypeStruct((owned, strip, TILE), f32),
         ),
         in_specs=[pl.BlockSpec(memory_space=pltpu.HBM)] * 3,
-        out_specs=(pl.BlockSpec(memory_space=pl.ANY), vmem),
+        out_specs=(pl.BlockSpec(memory_space=pl.ANY), pl.BlockSpec(memory_space=pl.ANY)),
         scratch_shapes=[
             pltpu.VMEM((rows, cols), f32),
             pltpu.SMEM(tile_owner.shape, jnp.int32),
@@ -448,19 +462,21 @@
             pltpu.VMEM((n_slab, 8, 128), f32),
             pltpu.VMEM((rows, cols), f32),
             pltpu.VMEM((cols // TILE, rows, TILE), f32),
-            pltpu.VMEM((n_layer // 2, n_slab, rows, TILE), f32),
-            pltpu.VMEM((n_layer // 2, n_slab, rows, TILE), f32),
+            pltpu.VMEM((ITERS, n_layer // 2, n_slab, rows, TILE), f32),
+            pltpu.VMEM((ITERS, n_layer // 2, n_slab, rows, TILE), f32),
+            pltpu.VMEM((n_slab, rows, TILE), f32),
+            pltpu.VMEM((owned, strip, TILE), f32),
             pltpu.SMEM((n_slab,), jnp.int32),
             pltpu.SemaphoreType.DMA((4, 4, CHUNKS)),
             pltpu.SemaphoreType.DMA((4, 4, CHUNKS)),
             pltpu.SemaphoreType.DMA((2, max(n_slab, n_layer))),
             pltpu.SemaphoreType.DMA((2, max(n_slab, n_layer))),
-            pltpu.SemaphoreType.DMA((n_layer // 2 * n_slab,)),
-            pltpu.SemaphoreType.DMA((n_layer // 2 * n_slab,)),
+            pltpu.SemaphoreType.DMA((ITERS, n_layer // 2 * n_slab)),
+            pltpu.SemaphoreType.DMA((ITERS, n_layer // 2 * n_slab)),
             pltpu.SemaphoreType.DMA((3,)),
         ],
         compiler_params=pltpu.CompilerParams(
-            collective_id=0, has_side_effects=True, vmem_limit_bytes=48 * 1024 * 1024
+            collective_id=0, has_side_effects=True, vmem_limit_bytes=63 * 1024 * 1024
         ),
         name="stack_cg",
     )(adjoint_source, conductivity, tile_owner)

time: 41.4 us -> 33.7 us (0.81)
  Pallas kernels: 36.7 us -> 30.5 us
  local copies, waits for them, and re-layouts: 3.88 us -> 2.34 us
    pallas_call x1, Pallas kernels: 36.7 us -> 30.5 us  [per_device(): pl.pallas_call(functools.partial(kernel, n_slab, n_layer), out_shape=(jax...]
    unnamed x8 -> x4, local copies, waits for them, and re-layouts: 3.88 us -> 2.34 us
where the time goes in v4:
time: 33.7 us; the launch traced here: 33.5 us
  Pallas kernels  30.5 us (91%)
  local copies, waits for them, and re-layouts  2.34 us (7%)
  between operations  0.65 us (2%)
    pallas_call x1, Pallas kernels, per_device(): pl.pallas_call(functools.partial(kernel, n_slab, n_layer), out_shape=(jax...  30.5 us
    unnamed x4, local copies, waits for them, and re-layouts  2.34 us

profile of v4, /device:TPU:0, one launch (start us, length us, event | category | flops | bytes accessed | tf_op | source)
XLA Modules:
  0.0 33.5 jit_solution(12129085757927150670)
XLA Ops:
  0.6 30.5 %stack_cg.1 = (f32[1,16,4096]{2,1,0:T(8,128)}, f32[4,32,128]{2,1,0:T(8,128)}) custom-call(f32[1,16,4096]{2,1,0:T(8,128)} %src_hbm.1, f32[1,16,4096]{2,1,0:T(8,128)} %cond_hbm.1, s32[1,32]{1,0:T(1,128)} %owner_hbm.1), custom_call_target="tpu_custom_call" | custom-call | tf_op jit(solution)/shard_map/stack_cg/pallas_call | solution.py:444
  31.2 0.0 copy-start
  31.2 1.7 %copy.7 = f32[1,16,4096]{2,1,0:T(8,128)} copy(f32[1,16,4096]{2,1,0:T(8,128)} %get-tuple-element.4) | data formatting | bytes 524288
  32.9 0.0 copy-done
  32.9 0.6 %copy.8 = f32[4,32,128]{2,1,0:T(8,128)} copy(f32[4,32,128]{2,1,0:T(8,128)S(1)} %copy-done) | data formatting | bytes 131072
Async XLA Ops:
  31.2 1.7 %copy-start = (f32[4,32,128]{2,1,0:T(8,128)S(1)}, f32[4,32,128]{2,1,0:T(8,128)}, u32[]{:S(2)}) copy-start(f32[4,32,128]{2,1,0:T(8,128)} %get-tuple-element.5) | copy-start | bytes 196612

commit v5 on v4

--- a/solution.py
+++ b/solution.py
@@ -10,6 +10,7 @@
 TILE = 128
 ITERS = 3
 CHUNKS = 4
+ROW_CHUNKS = 2
 PAD = 128
 MESH = pl.DeviceIdType.MESH
 
@@ -94,6 +95,7 @@
     layer = lax.axis_index("layer")
     rows, cols = src_ref.shape
     width = cols // CHUNKS
+    per_row = CHUNKS // ROW_CHUNKS
     top, bottom = 8, 8 + rows
     tile_rows, tiles_across = owner_ref.shape
     strip = TILE // n_layer
@@ -161,8 +163,8 @@
         @pl.when(axis_end)
         def _():
             for s in range(4):
-                for j in range(CHUNKS):
-                    row_recv[s, d, j] = jnp.zeros((1, width), jnp.float32)
+                for j in range(ROW_CHUNKS):
+                    row_recv[s, d, j] = jnp.zeros((1, cols // ROW_CHUNKS), jnp.float32)
 
     sends_to = (layer < n_layer - 1, layer > 0, slab < n_slab - 1, slab > 0)
     gets_from = (layer > 0, layer < n_layer - 1, slab > 0, slab < n_slab - 1)
@@ -187,29 +189,37 @@
 
     def halo_copy(stage, direction, j):
         span = pl.ds(j * width, width)
+        slot = j if direction < 2 else j // per_row
         if direction < 2:
             source = fields.at[stage, pl.ds(top, rows), pl.ds(PAD + j * width, width)]
             dest = layer_halo.at[stage, direction, :, span]
         else:
-            source = row_send.at[stage, direction - 2, j]
-            dest = row_recv.at[stage, direction - 2, j]
+            source = row_send.at[stage, direction - 2, j // per_row]
+            dest = row_recv.at[stage, direction - 2, j // per_row]
         return pltpu.make_async_remote_copy(
             src_ref=source,
             dst_ref=dest,
-            send_sem=halo_ssem.at[stage, direction, j],
-            recv_sem=halo_rsem.at[stage, direction, j],
+            send_sem=halo_ssem.at[stage, direction, slot],
+            recv_sem=halo_rsem.at[stage, direction, slot],
             device_id=target[direction],
             device_id_type=MESH,
         )
 
     def put_field(stage, j, value):
         fields[stage, top:bottom, PAD + j * width : PAD + (j + 1) * width] = value
-        row_send[stage, 0, j] = value[rows - 1 : rows]
-        row_send[stage, 1, j] = value[0:1]
+        part = slice((j % per_row) * width, (j % per_row + 1) * width)
+        row_send[stage, 0, j // per_row, :, part] = value[rows - 1 : rows]
+        row_send[stage, 1, j // per_row, :, part] = value[0:1]
+
+    def sent_with(stage, direction, j):
+        return used(stage, direction, j) and (direction < 2 or j % per_row == per_row - 1)
+
+    def got_with(stage, direction, j):
+        return used(stage, direction, j) and (direction < 2 or j % per_row == 0)
 
     def send_field(stage, j):
         for direction in range(4):
-            if used(stage, direction, j):
+            if sent_with(stage, direction, j):
 
                 @pl.when(sends_to[direction] & wanted(stage, direction, j, layer))
                 def _():
@@ -217,16 +227,17 @@
 
     def get_halo(stage, j):
         for direction in range(4):
-            if used(stage, direction, j):
+            if got_with(stage, direction, j):
 
                 @pl.when(gets_from[direction] & wanted(stage, direction, j, layer + 1))
                 def _():
                     halo_copy(stage, direction, j).wait_recv()
 
         span = slice(PAD + j * width, PAD + (j + 1) * width)
-        fields[stage, top - 1 : top, span] = row_recv[stage, 0, j]
+        part = slice((j % per_row) * width, (j % per_row + 1) * width)
+        fields[stage, top - 1 : top, span] = row_recv[stage, 0, j // per_row, :, part]
         if stage < 3:
-            fields[stage, bottom : bottom + 1, span] = row_recv[stage, 1, j]
+            fields[stage, bottom : bottom + 1, span] = row_recv[stage, 1, j // per_row, :, part]
 
     def near(stage, j, which):
         c0 = j * width
@@ -250,8 +261,10 @@
 
     cond_copy.wait()
     for j in range(CHUNKS):
-        row_send[0, 0, j] = fields[0, bottom - 1 : bottom, PAD + j * width : PAD + (j + 1) * width]
-        row_send[0, 1, j] = fields[0, top : top + 1, PAD + j * width : PAD + (j + 1) * width]
+        part = slice((j % per_row) * width, (j % per_row + 1) * width)
+        span = slice(PAD + j * width, PAD + (j + 1) * width)
+        row_send[0, 0, j // per_row, :, part] = fields[0, bottom - 1 : bottom, span]
+        row_send[0, 1, j // per_row, :, part] = fields[0, top : top + 1, span]
     pl.semaphore_wait(barrier, n_greet)
     for j in range(CHUNKS):
         send_field(0, j)
@@ -376,6 +389,18 @@
     repeat(1, n_layer, lambda d: layer_sum_copy(d).wait_recv())
     red_slab[slab] = sum(red_layer[i] for i in range(n_layer))
     repeat(1, n_slab, lambda d: slab_sum_copy(d).start())
+    for stage in range(4):
+        for j in range(CHUNKS):
+            for direction in range(4):
+                if sent_with(stage, direction, j):
+
+                    @pl.when(sends_to[direction] & wanted(stage, direction, j, layer))
+                    def _():
+                        halo_copy(stage, direction, j).wait_send()
+    for k in range(ITERS - 1):
+        repeat(1, n_pair * n_slab, lambda n: tile_copy(k, n).wait_recv())
+        repeat(1, n_pair * n_slab, lambda n: tile_copy(k, n).wait_send())
+    repeat(1, n_layer, lambda d: layer_sum_copy(d).wait_send())
     repeat(1, n_slab, lambda d: slab_sum_copy(d).wait_recv())
     total = jnp.sum(sum(red_slab[i] for i in range(n_slab)), axis=1, keepdims=True)
     scales = [2.0 * c for c in cg_coefficients([total[k : k + 1] for k in range(6)])]
@@ -386,8 +411,7 @@
     x_copy = pltpu.make_async_copy(x_buf, x_out.at[0], local_sem.at[0])
     x_copy.start()
 
-    for k in range(ITERS):
-        repeat(1, n_pair * n_slab, lambda n: tile_copy(k, n).wait_recv())
+    repeat(1, n_pair * n_slab, lambda n: tile_copy(ITERS - 1, n).wait_recv())
 
     def combine(i, carry):
         value = None
@@ -417,19 +441,8 @@
     g_copy = pltpu.make_async_copy(g_buf, g_out, local_sem.at[1])
     g_copy.start()
 
-    for stage in range(4):
-        for j in range(CHUNKS):
-            for direction in range(4):
-                if used(stage, direction, j):
-
-                    @pl.when(sends_to[direction] & wanted(stage, direction, j, layer))
-                    def _():
-                        halo_copy(stage, direction, j).wait_send()
-
-    repeat(1, n_layer, lambda d: layer_sum_copy(d).wait_send())
     repeat(1, n_slab, lambda d: slab_sum_copy(d).wait_send())
-    for k in range(ITERS):
-        repeat(1, n_pair * n_slab, lambda n: tile_copy(k, n).wait_send())
+    repeat(1, n_pair * n_slab, lambda n: tile_copy(ITERS - 1, n).wait_send())
     x_copy.wait()
     g_copy.wait()
 
@@ -456,8 +469,8 @@
             pltpu.VMEM((6, rows, cols), f32),
             pltpu.VMEM((rows, cols), f32),
             pltpu.VMEM((4, 2, rows, cols), f32),
-            pltpu.VMEM((4, 2, CHUNKS, 1, width), f32),
-            pltpu.VMEM((4, 2, CHUNKS, 1, width), f32),
+            pltpu.VMEM((4, 2, ROW_CHUNKS, 1, cols // ROW_CHUNKS), f32),
+            pltpu.VMEM((4, 2, ROW_CHUNKS, 1, cols // ROW_CHUNKS), f32),
             pltpu.VMEM((n_layer, 8, 128), f32),
             pltpu.VMEM((n_slab, 8, 128), f32),
             pltpu.VMEM((rows, cols), f32),
@@ -476,10 +489,10 @@
             pltpu.SemaphoreType.DMA((3,)),
         ],
         compiler_params=pltpu.CompilerParams(
-            collective_id=0, has_side_effects=True, vmem_limit_bytes=63 * 1024 * 1024
+            collective_id=0, has_side_effects=True, vmem_limit_bytes=48 * 1024 * 1024
         ),
         name="stack_cg",
-    )(adjoint_source, conductivity, tile_owner)
+    )(*[pltpu.with_memory_space_constraint(v, pltpu.HBM) for v in (adjoint_source, conductivity, tile_owner)])
 
 
 def solution(mesh):

time: 33.7 us -> 32.6 us (0.967)
  local copies, waits for them, and re-layouts: 2.34 us -> 1.33 us
    unnamed x4 -> x2, local copies, waits for them, and re-layouts: 2.34 us -> 1.33 us
where the time goes in v5:
time: 32.6 us; the launch traced here: 32.4 us
  Pallas kernels  30.5 us (94%)
  local copies, waits for them, and re-layouts  1.33 us (4%)
  between operations  0.64 us (2%)
    pallas_call x1, Pallas kernels, per_device(): pl.pallas_call(functools.partial(kernel, n_slab, n_layer), out_shape=(jax...  30.5 us
    unnamed x2, local copies, waits for them, and re-layouts  1.33 us

profile of v5, /device:TPU:0, one launch (start us, length us, event | category | flops | bytes accessed | tf_op | source)
XLA Modules:
  0.0 32.4 jit_solution(9213650732105627539)
XLA Ops:
  0.6 30.5 %stack_cg.1 = (f32[1,16,4096]{2,1,0:T(8,128)S(1)}, f32[4,32,128]{2,1,0:T(8,128)S(1)}) custom-call(f32[1,16,4096]{2,1,0:T(8,128)} %src_hbm.1, f32[1,16,4096]{2,1,0:T(8,128)} %cond_hbm.1, s32[1,32]{1,0:T(1,128)} %owner_hbm.1), custom_call_target="tpu_custom_call" | custom-call | tf_op jit(solution)/shard_map/stack_cg/pallas_call | solution.py:457
  31.1 0.7 %copy.7 = f32[1,16,4096]{2,1,0:T(8,128)} copy(f32[1,16,4096]{2,1,0:T(8,128)S(1)} %get-tuple-element.4) | data formatting | bytes 524288
  31.8 0.6 %copy.8 = f32[4,32,128]{2,1,0:T(8,128)} copy(f32[4,32,128]{2,1,0:T(8,128)S(1)} %get-tuple-element.5) | data formatting | bytes 131072

commit v6 on v5

--- a/solution.py
+++ b/solution.py
@@ -320,7 +320,7 @@
             for t in range(width // TILE):
                 x_tiles[j * (width // TILE) + t] = value[:, t * TILE : (t + 1) * TILE]
 
-        def pack(owner, carry):
+        def pack(owner):
             packed = table[owner]
             pieces = [None] * n_pair
             for q in range(capacity):
@@ -333,9 +333,8 @@
                     pieces[p] = moved if q == 0 else jnp.where(lane == q, moved, pieces[p])
             for p in range(n_pair):
                 tile_send[k, p, owner] = pieces[p]
-            return carry
-
-        lax.fori_loop(0, n_slab, pack, 0)
+
+        repeat(0, n_slab, pack)
         repeat(1, n_pair * n_slab, lambda n: tile_copy(k, n).start())
         tile_recv[k, pair, slab] = tile_send[k, pair, slab]
 
@@ -413,15 +412,14 @@
 
     repeat(1, n_pair * n_slab, lambda n: tile_copy(ITERS - 1, n).wait_recv())
 
-    def combine(i, carry):
+    def combine(i):
         value = None
         for k in range(ITERS):
             term = scales[k] * sum(tile_recv[k, p, i] for p in range(n_pair))
             value = term if value is None else value + term
         tiles[i] = value
-        return carry
-
-    lax.fori_loop(0, n_slab, combine, 0)
+
+    repeat(0, n_slab, combine)
     if tile_rows == 1:
         turned = jnp.transpose(tiles[...].reshape(TILE, TILE))
         for k in range(owned_count):

time: 32.6 us -> 31.7 us (0.972)
  Pallas kernels: 30.5 us -> 29.6 us
    pallas_call x1, Pallas kernels: 30.5 us -> 29.6 us  [per_device(): pl.pallas_call(functools.partial(kernel, n_slab, n_layer), out_shape=(jax...]
where the time goes in v6:
time: 31.7 us; the launch traced here: 31.6 us
  Pallas kernels  29.6 us (93%)
  local copies, waits for them, and re-layouts  1.33 us (4%)
  between operations  0.64 us (2%)
    pallas_call x1, Pallas kernels, per_device(): pl.pallas_call(functools.partial(kernel, n_slab, n_layer), out_shape=(jax...  29.6 us
    unnamed x2, local copies, waits for them, and re-layouts  1.33 us

profile of v6, /device:TPU:0, one launch (start us, length us, event | category | flops | bytes accessed | tf_op | source)
XLA Modules:
  0.0 31.6 jit_solution(4928775856847534835)
XLA Ops:
  0.6 29.6 %stack_cg.1 = (f32[1,16,4096]{2,1,0:T(8,128)S(1)}, f32[4,32,128]{2,1,0:T(8,128)S(1)}) custom-call(f32[1,16,4096]{2,1,0:T(8,128)} %src_hbm.1, f32[1,16,4096]{2,1,0:T(8,128)} %cond_hbm.1, s32[1,32]{1,0:T(1,128)} %owner_hbm.1), custom_call_target="tpu_custom_call" | custom-call | tf_op jit(solution)/shard_map/stack_cg/pallas_call | solution.py:455
  30.2 0.7 %copy.7 = f32[1,16,4096]{2,1,0:T(8,128)} copy(f32[1,16,4096]{2,1,0:T(8,128)S(1)} %get-tuple-element.4) | data formatting | bytes 524288
  31.0 0.6 %copy.8 = f32[4,32,128]{2,1,0:T(8,128)} copy(f32[4,32,128]{2,1,0:T(8,128)S(1)} %get-tuple-element.5) | data formatting | bytes 131072

commit v7 on v6

--- a/solution.py
+++ b/solution.py
@@ -74,8 +74,7 @@
     layer_halo,
     row_send,
     row_recv,
-    red_layer,
-    red_slab,
+    sums,
     x_buf,
     x_tiles,
     tile_send,
@@ -85,8 +84,8 @@
     table,
     halo_ssem,
     halo_rsem,
-    red_ssem,
-    red_rsem,
+    sum_ssem,
+    sum_rsem,
     tile_ssem,
     tile_rsem,
     local_sem,
@@ -109,11 +108,8 @@
     def turn(me, d, count):
         return lax.rem(me + d, count)
 
-    def layer_peer(d):
-        return {"layer": turn(layer, d, n_layer)}
-
-    def slab_peer(d):
-        return {"slab": turn(slab, d, n_slab)}
+    def any_peer(n):
+        return {"layer": turn(layer, n // n_slab, n_layer), "slab": turn(slab, n % n_slab, n_slab)}
 
     def tile_peer(n):
         to_pair, to_slab = turn(pair, n // n_slab, n_pair), turn(slab, n % n_slab, n_slab)
@@ -131,13 +127,8 @@
     def greet(device):
         pl.semaphore_signal(barrier, inc=1, device_id=device, device_id_type=MESH)
 
-    n_greet = 0
-    for d in range(1, n_layer):
-        if d % 2 == 1:
-            greet(layer_peer(d))
-            n_greet += 1
-    repeat(1, n_pair * n_slab, lambda n: greet(tile_peer(n)[2]))
-    n_greet += n_pair * n_slab - 1
+    n_greet = n_layer * n_slab - 1
+    repeat(1, n_greet + 1, lambda n: greet(any_peer(n)))
 
     cond_copy = pltpu.make_async_copy(
         cond_hbm.at[0], fields.at[0, pl.ds(top, rows), pl.ds(PAD, cols)], local_sem.at[0]
@@ -281,25 +272,25 @@
 
     lax.fori_loop(0, n_slab, list_tiles, 0)
 
-    def layer_sum_copy(d):
+    def sum_copy(n):
         return pltpu.make_async_remote_copy(
-            src_ref=red_layer.at[layer],
-            dst_ref=red_layer.at[layer],
-            send_sem=red_ssem.at[0, d],
-            recv_sem=red_rsem.at[0, d],
-            device_id=layer_peer(d),
+            src_ref=sums.at[layer * n_slab + slab],
+            dst_ref=sums.at[layer * n_slab + slab],
+            send_sem=sum_ssem,
+            recv_sem=sum_rsem,
+            device_id=any_peer(n),
             device_id_type=MESH,
         )
 
-    def slab_sum_copy(d):
-        return pltpu.make_async_remote_copy(
-            src_ref=red_slab.at[slab],
-            dst_ref=red_slab.at[slab],
-            send_sem=red_ssem.at[1, d],
-            recv_sem=red_rsem.at[1, d],
-            device_id=slab_peer(d),
-            device_id_type=MESH,
-        )
+    others = pl.ds(0, n_layer * n_slab - 1)
+    all_sums = pltpu.make_async_remote_copy(
+        src_ref=sums.at[others],
+        dst_ref=sums.at[others],
+        send_sem=sum_ssem,
+        recv_sem=sum_rsem,
+        device_id=any_peer(1),
+        device_id_type=MESH,
+    )
 
     def tile_copy(k, n):
         to_pair, to_slab, device = tile_peer(n)
@@ -381,13 +372,14 @@
         moments[5] = moments[5] + fold(here(3, j) * image)
     moments[5] = 2.0 * moments[5]
 
-    sums = [jnp.sum(m, axis=0, keepdims=True) for m in moments]
-    red_layer[layer] = jnp.concatenate(sums + [jnp.zeros((2, 128), jnp.float32)], axis=0)
-    repeat(1, n_layer, lambda d: layer_sum_copy(d).start())
+    own_sums = jnp.zeros((1, 128), jnp.float32)
+    place = lax.broadcasted_iota(jnp.int32, (1, 128), 1)
+    for k in range(6):
+        own = jnp.sum(jnp.sum(moments[k], axis=0, keepdims=True), axis=1, keepdims=True)
+        own_sums = jnp.where(place == k, own, own_sums)
+    sums[layer * n_slab + slab] = own_sums
+    repeat(1, n_layer * n_slab, lambda n: sum_copy(n).start())
     deliver(2)
-    repeat(1, n_layer, lambda d: layer_sum_copy(d).wait_recv())
-    red_slab[slab] = sum(red_layer[i] for i in range(n_layer))
-    repeat(1, n_slab, lambda d: slab_sum_copy(d).start())
     for stage in range(4):
         for j in range(CHUNKS):
             for direction in range(4):
@@ -399,10 +391,9 @@
     for k in range(ITERS - 1):
         repeat(1, n_pair * n_slab, lambda n: tile_copy(k, n).wait_recv())
         repeat(1, n_pair * n_slab, lambda n: tile_copy(k, n).wait_send())
-    repeat(1, n_layer, lambda d: layer_sum_copy(d).wait_send())
-    repeat(1, n_slab, lambda d: slab_sum_copy(d).wait_recv())
-    total = jnp.sum(sum(red_slab[i] for i in range(n_slab)), axis=1, keepdims=True)
-    scales = [2.0 * c for c in cg_coefficients([total[k : k + 1] for k in range(6)])]
+    all_sums.wait_recv()
+    total = jnp.sum(sums[...], axis=0)
+    scales = [2.0 * c for c in cg_coefficients([total[:, k : k + 1] for k in range(6)])]
 
     for j in range(CHUNKS):
         value = scales[0] * here(1, j) + scales[1] * here(2, j) + scales[2] * here(3, j)
@@ -439,7 +430,7 @@
     g_copy = pltpu.make_async_copy(g_buf, g_out, local_sem.at[1])
     g_copy.start()
 
-    repeat(1, n_slab, lambda d: slab_sum_copy(d).wait_send())
+    all_sums.wait_send()
     repeat(1, n_pair * n_slab, lambda n: tile_copy(ITERS - 1, n).wait_send())
     x_copy.wait()
     g_copy.wait()
@@ -469,8 +460,7 @@
             pltpu.VMEM((4, 2, rows, cols), f32),
             pltpu.VMEM((4, 2, ROW_CHUNKS, 1, cols // ROW_CHUNKS), f32),
             pltpu.VMEM((4, 2, ROW_CHUNKS, 1, cols // ROW_CHUNKS), f32),
-            pltpu.VMEM((n_layer, 8, 128), f32),
-            pltpu.VMEM((n_slab, 8, 128), f32),
+            pltpu.VMEM((n_layer * n_slab, 1, 128), f32),
             pltpu.VMEM((rows, cols), f32),
             pltpu.VMEM((cols // TILE, rows, TILE), f32),
             pltpu.VMEM((ITERS, n_layer // 2, n_slab, rows, TILE), f32),
@@ -480,8 +470,8 @@
             pltpu.SMEM((n_slab,), jnp.int32),
             pltpu.SemaphoreType.DMA((4, 4, CHUNKS)),
             pltpu.SemaphoreType.DMA((4, 4, CHUNKS)),
-            pltpu.SemaphoreType.DMA((2, max(n_slab, n_layer))),
-            pltpu.SemaphoreType.DMA((2, max(n_slab, n_layer))),
+            pltpu.SemaphoreType.DMA,
+            pltpu.SemaphoreType.DMA,
             pltpu.SemaphoreType.DMA((ITERS, n_layer // 2 * n_slab)),
             pltpu.SemaphoreType.DMA((ITERS, n_layer // 2 * n_slab)),
             pltpu.SemaphoreType.DMA((3,)),

time: 31.7 us -> 30.8 us (0.972)
  Pallas kernels: 29.6 us -> 28.7 us
    pallas_call x1, Pallas kernels: 29.6 us -> 28.7 us  [per_device(): pl.pallas_call(functools.partial(kernel, n_slab, n_layer), out_shape=(jax...]
where the time goes in v7:
time: 30.8 us; the launch traced here: 30.7 us
  Pallas kernels  28.7 us (93%)
  local copies, waits for them, and re-layouts  1.33 us (4%)
  between operations  0.64 us (2%)
    pallas_call x1, Pallas kernels, per_device(): pl.pallas_call(functools.partial(kernel, n_slab, n_layer), out_shape=(jax...  28.7 us
    unnamed x2, local copies, waits for them, and re-layouts  1.33 us

profile of v7, /device:TPU:0, one launch (start us, length us, event | category | flops | bytes accessed | tf_op | source)
XLA Modules:
  0.0 30.7 jit_solution(936009407796903847)
XLA Ops:
  0.6 28.7 %stack_cg.1 = (f32[1,16,4096]{2,1,0:T(8,128)S(1)}, f32[4,32,128]{2,1,0:T(8,128)S(1)}) custom-call(f32[1,16,4096]{2,1,0:T(8,128)} %src_hbm.1, f32[1,16,4096]{2,1,0:T(8,128)} %cond_hbm.1, s32[1,32]{1,0:T(1,128)} %owner_hbm.1), custom_call_target="tpu_custom_call" | custom-call | tf_op jit(solution)/shard_map/stack_cg/pallas_call | solution.py:446
  29.4 0.7 %copy.7 = f32[1,16,4096]{2,1,0:T(8,128)} copy(f32[1,16,4096]{2,1,0:T(8,128)S(1)} %get-tuple-element.4) | data formatting | bytes 524288
  30.1 0.6 %copy.8 = f32[4,32,128]{2,1,0:T(8,128)} copy(f32[4,32,128]{2,1,0:T(8,128)S(1)} %get-tuple-element.5) | data formatting | bytes 131072

commit v8 on v7

--- a/solution.py
+++ b/solution.py
@@ -292,13 +292,24 @@
         device_id_type=MESH,
     )
 
+    def all_tiles(k):
+        other_tiles = pl.ds(0, n_pair * n_slab - 1)
+        return pltpu.make_async_remote_copy(
+            src_ref=tile_send.at[k, other_tiles],
+            dst_ref=tile_recv.at[k, other_tiles],
+            send_sem=tile_ssem.at[k],
+            recv_sem=tile_rsem.at[k],
+            device_id=tile_peer(1)[2],
+            device_id_type=MESH,
+        )
+
     def tile_copy(k, n):
         to_pair, to_slab, device = tile_peer(n)
         return pltpu.make_async_remote_copy(
-            src_ref=tile_send.at[k, to_pair, to_slab],
-            dst_ref=tile_recv.at[k, pair, slab],
-            send_sem=tile_ssem.at[k, n],
-            recv_sem=tile_rsem.at[k, n],
+            src_ref=tile_send.at[k, to_pair * n_slab + to_slab],
+            dst_ref=tile_recv.at[k, pair * n_slab + slab],
+            send_sem=tile_ssem.at[k],
+            recv_sem=tile_rsem.at[k],
             device_id=device,
             device_id_type=MESH,
         )
@@ -323,11 +334,11 @@
                     moved = tile if shift == 0 else pltpu.roll(tile, shift, 1)
                     pieces[p] = moved if q == 0 else jnp.where(lane == q, moved, pieces[p])
             for p in range(n_pair):
-                tile_send[k, p, owner] = pieces[p]
+                tile_send[k, p * n_slab + owner] = pieces[p]
 
         repeat(0, n_slab, pack)
         repeat(1, n_pair * n_slab, lambda n: tile_copy(k, n).start())
-        tile_recv[k, pair, slab] = tile_send[k, pair, slab]
+        tile_recv[k, pair * n_slab + slab] = tile_send[k, pair * n_slab + slab]
 
     src_copy.wait()
     moments = [jnp.zeros((8, 128), jnp.float32) for _ in range(6)]
@@ -389,8 +400,8 @@
                     def _():
                         halo_copy(stage, direction, j).wait_send()
     for k in range(ITERS - 1):
-        repeat(1, n_pair * n_slab, lambda n: tile_copy(k, n).wait_recv())
-        repeat(1, n_pair * n_slab, lambda n: tile_copy(k, n).wait_send())
+        all_tiles(k).wait_recv()
+        all_tiles(k).wait_send()
     all_sums.wait_recv()
     total = jnp.sum(sums[...], axis=0)
     scales = [2.0 * c for c in cg_coefficients([total[:, k : k + 1] for k in range(6)])]
@@ -401,12 +412,12 @@
     x_copy = pltpu.make_async_copy(x_buf, x_out.at[0], local_sem.at[0])
     x_copy.start()
 
-    repeat(1, n_pair * n_slab, lambda n: tile_copy(ITERS - 1, n).wait_recv())
+    all_tiles(ITERS - 1).wait_recv()
 
     def combine(i):
         value = None
         for k in range(ITERS):
-            term = scales[k] * sum(tile_recv[k, p, i] for p in range(n_pair))
+            term = scales[k] * sum(tile_recv[k, p * n_slab + i] for p in range(n_pair))
             value = term if value is None else value + term
         tiles[i] = value
 
@@ -431,7 +442,7 @@
     g_copy.start()
 
     all_sums.wait_send()
-    repeat(1, n_pair * n_slab, lambda n: tile_copy(ITERS - 1, n).wait_send())
+    all_tiles(ITERS - 1).wait_send()
     x_copy.wait()
     g_copy.wait()
 
@@ -463,8 +474,8 @@
             pltpu.VMEM((n_layer * n_slab, 1, 128), f32),
             pltpu.VMEM((rows, cols), f32),
             pltpu.VMEM((cols // TILE, rows, TILE), f32),
-            pltpu.VMEM((ITERS, n_layer // 2, n_slab, rows, TILE), f32),
-            pltpu.VMEM((ITERS, n_layer // 2, n_slab, rows, TILE), f32),
+            pltpu.VMEM((ITERS, n_layer // 2 * n_slab, rows, TILE), f32),
+            pltpu.VMEM((ITERS, n_layer // 2 * n_slab, rows, TILE), f32),
             pltpu.VMEM((n_slab, rows, TILE), f32),
             pltpu.VMEM((owned, strip, TILE), f32),
             pltpu.SMEM((n_slab,), jnp.int32),
@@ -472,8 +483,8 @@
             pltpu.SemaphoreType.DMA((4, 4, CHUNKS)),
             pltpu.SemaphoreType.DMA,
             pltpu.SemaphoreType.DMA,
-            pltpu.SemaphoreType.DMA((ITERS, n_layer // 2 * n_slab)),
-            pltpu.SemaphoreType.DMA((ITERS, n_layer // 2 * n_slab)),
+            pltpu.SemaphoreType.DMA((ITERS,)),
+            pltpu.SemaphoreType.DMA((ITERS,)),
             pltpu.SemaphoreType.DMA((3,)),
         ],
         compiler_params=pltpu.CompilerParams(

time: 30.8 us -> 30 us (0.974)
  Pallas kernels: 28.7 us -> 27.9 us
    pallas_call x1, Pallas kernels: 28.7 us -> 27.9 us  [per_device(): pl.pallas_call(functools.partial(kernel, n_slab, n_layer), out_shape=(jax...]
where the time goes in v8:
time: 30 us; the launch traced here: 29.9 us
  Pallas kernels  27.9 us (93%)
  local copies, waits for them, and re-layouts  1.33 us (4%)
  between operations  0.64 us (2%)
    pallas_call x1, Pallas kernels, per_device(): pl.pallas_call(functools.partial(kernel, n_slab, n_layer), out_shape=(jax...  27.9 us
    unnamed x2, local copies, waits for them, and re-layouts  1.33 us

profile of v8, /device:TPU:0, one launch (start us, length us, event | category | flops | bytes accessed | tf_op | source)
XLA Modules:
  0.0 29.9 jit_solution(12313868029536992633)
XLA Ops:
  0.6 27.9 %stack_cg.1 = (f32[1,16,4096]{2,1,0:T(8,128)S(1)}, f32[4,32,128]{2,1,0:T(8,128)S(1)}) custom-call(f32[1,16,4096]{2,1,0:T(8,128)} %src_hbm.1, f32[1,16,4096]{2,1,0:T(8,128)} %cond_hbm.1, s32[1,32]{1,0:T(1,128)} %owner_hbm.1), custom_call_target="tpu_custom_call" | custom-call | tf_op jit(solution)/shard_map/stack_cg/pallas_call | solution.py:457
  28.5 0.7 %copy.7 = f32[1,16,4096]{2,1,0:T(8,128)} copy(f32[1,16,4096]{2,1,0:T(8,128)S(1)} %get-tuple-element.4) | data formatting | bytes 524288
  29.2 0.6 %copy.8 = f32[4,32,128]{2,1,0:T(8,128)} copy(f32[4,32,128]{2,1,0:T(8,128)S(1)} %get-tuple-element.5) | data formatting | bytes 131072
